TPU v7x, 32 devices: a whole 2x2x4 slice. The times are simulated.
32 devices in a mesh: dp: 8 (over y, x, core), seq: 4 (over z).
Axes of the slice: x: 2, y: 2, z: 4, core: 2. Of those that a mesh axis runs over, the one named last changes fastest.
Arguments:
- tokens: bfloat16 [16384, 768], P(('dp', 'seq')), may hold values from -6 to 6
- w_qkv: bfloat16 [768, 2304], P(('dp', 'seq')), may hold values from -0.21875 to 0.21875
- w_out: bfloat16 [768, 768], P(('dp', 'seq')), may hold values from -1.75 to 1.75
- attn_gain: bfloat16 [768], P(('dp', 'seq')), may hold values from 0.5 to 1.5
- mlp_gain: bfloat16 [768], P(('dp', 'seq')), may hold values from 0.5 to 1.5
- w_in: bfloat16 [768, 2, 1152], P('dp', None, 'seq'), may hold values from -0.21875 to 0.21875
- w_down: bfloat16 [1152, 768], P('seq', 'dp'), may hold values from -0.1875 to 0.1875
- grad_out: bfloat16 [16384, 768], P(('dp', 'seq')), may hold values from -6 to 6
Outputs:
- out_block: bfloat16 [16384, 768], P(('dp', 'seq'))
- grad_tokens: bfloat16 [16384, 768], P(('dp', 'seq'))
- grad_w_qkv: float32 [768, 2304], P(('dp', 'seq'))
- grad_w_out: float32 [768, 768], P(('dp', 'seq'))
- grad_attn_gain: float32 [768], P(('dp', 'seq'))
- grad_mlp_gain: float32 [768], P(('dp', 'seq'))
- grad_w_in: float32 [768, 2, 1152], P('dp', None, 'seq')
- grad_w_down: float32 [1152, 768], P('seq', 'dp')
All inputs are finite; a program needn't handle non-finite values.
Results may differ from a plain program's by a relative error of at most 0.028.
Values may be sent and summed in bfloat16 or wider, within the bound.
A program may use at most 128 MiB of HBM per device.

v0:
```python
import jax
import jax.numpy as jnp
from jax import lax
from jax.sharding import PartitionSpec as P

HEADS = 12
HEAD_DIM = 64


NORM_EPS = 1e-05
ROPE_THETA = 160000.0


def split_up(shard, dim, size):
    before, after = (shard.shape[:dim], shard.shape[dim + 1 :])
    return jnp.moveaxis(shard.reshape(*before, size, -1, *after), dim, 0)


def sent_and_summed(shard, axis, dim):
    size = lax.axis_size(axis)
    tiles = lax.all_to_all(split_up(shard, dim, size), axis, 0, 0, tiled=True)
    return jnp.sum(tiles.astype(jnp.float32), axis=0)


def norm_rows(values, gain):
    mean_row = jnp.mean(values, -1, keepdims=True)
    centred = values - mean_row
    inv_std = lax.rsqrt(jnp.mean(centred * centred, -1, keepdims=True) + NORM_EPS)
    normed = centred * inv_std
    return (normed * gain, normed, inv_std)


def norm_back(grad_y, gain, normed, inv_std):
    grad_hat = grad_y * gain
    grad_in = inv_std * (
        grad_hat
        - jnp.mean(grad_hat, -1, keepdims=True)
        - normed * jnp.mean(grad_hat * normed, -1, keepdims=True)
    )
    return (grad_in, jnp.sum(grad_y * normed, 0))


def rotary_tables(first_pos, pos_count, head_size):
    position = (first_pos + jnp.arange(pos_count)).astype(jnp.float32)
    half_dim = head_size // 2
    inv_freq = ROPE_THETA ** (-jnp.arange(half_dim).astype(jnp.float32) * 2.0 / head_size)
    angle_tab = position[:, None] * inv_freq[None, :]
    angle_tab = jnp.concatenate([angle_tab, angle_tab], -1)
    return (jnp.cos(angle_tab), jnp.sin(angle_tab))


def rotate(values, cos_tab, sine_tab):
    half_dim = values.shape[-1] // 2
    turned = jnp.concatenate([-values[..., half_dim:], values[..., :half_dim]], -1)
    return values * cos_tab[:, None, :] + turned * sine_tab[:, None, :]


def rotate_back(gradient, cos_tab, sine_tab):
    half_dim = gradient.shape[-1] // 2
    scaled = gradient * sine_tab[:, None, :]
    back_part = jnp.concatenate([scaled[..., half_dim:], -scaled[..., :half_dim]], -1)
    return gradient * cos_tab[:, None, :] + back_part


def split_pairs(matrix):
    return matrix.reshape(matrix.shape[0], HEADS // 2, 2, HEAD_DIM).transpose(1, 0, 2, 3)


def join_pairs(stacked):
    return stacked.transpose(1, 0, 2, 3).reshape(stacked.shape[1], HEADS * HEAD_DIM)


def attend(pieces):
    query_pair, key_pair, value_pair = pieces
    scores = jnp.einsum(
        "qhd,khd->hqk", query_pair, key_pair, preferred_element_type=jnp.float32
    ) * HEAD_DIM ** (-0.5)
    row_top = jnp.max(scores, -1, keepdims=True)
    expo_vals = jnp.exp(scores - row_top)
    row_total = jnp.sum(expo_vals, -1, keepdims=True)
    prob_vals = (expo_vals / row_total).astype(jnp.bfloat16)
    result = jnp.einsum("hqk,khd->qhd", prob_vals, value_pair, preferred_element_type=jnp.float32)
    return (result, (row_top + jnp.log(row_total))[..., 0])


def attend_back(pieces):
    query_pair, key_pair, value_pair, grad_pair, log_total = pieces
    scale_qk = HEAD_DIM ** (-0.5)
    scores = (
        jnp.einsum("qhd,khd->hqk", query_pair, key_pair, preferred_element_type=jnp.float32)
        * scale_qk
    )
    prob_vals = jnp.exp(scores - log_total[..., None])
    grad_probs = jnp.einsum(
        "qhd,khd->hqk", grad_pair, value_pair, preferred_element_type=jnp.float32
    )
    grad_value = jnp.einsum(
        "hqk,qhd->khd",
        prob_vals.astype(jnp.bfloat16),
        grad_pair,
        preferred_element_type=jnp.float32,
    )
    grad_scores = (
        prob_vals * (grad_probs - jnp.sum(prob_vals * grad_probs, -1, keepdims=True))
    ).astype(jnp.bfloat16)
    grad_query = (
        jnp.einsum("hqk,khd->qhd", grad_scores, key_pair, preferred_element_type=jnp.float32)
        * scale_qk
    )
    grad_key = (
        jnp.einsum("hqk,qhd->khd", grad_scores, query_pair, preferred_element_type=jnp.float32)
        * scale_qk
    )
    return (grad_query, grad_key, grad_value)


def geglu(gate_in, up_in):
    return jax.nn.gelu(gate_in, approximate=False) * up_in


def on_device(tokens, w_qkv, w_out, attn_gain, mlp_gain, w_in, w_down, grad_out):
    row_count = tokens.shape[0]
    model_width = tokens.shape[1]
    full_qkv, full_out, gain_a, gain_m = (
        lax.all_gather(w_qkv, ("dp", "seq"), axis=0, tiled=True),
        lax.all_gather(w_out, ("dp", "seq"), axis=0, tiled=True),
        lax.all_gather(attn_gain, ("dp", "seq"), axis=0, tiled=True),
        lax.all_gather(mlp_gain, ("dp", "seq"), axis=0, tiled=True),
    )
    gain_a = gain_a.astype(jnp.float32)
    gain_m = gain_m.astype(jnp.float32)
    local_in, local_down = (
        lax.all_gather(w_in, "dp", axis=0, tiled=True),
        lax.all_gather(w_down, "dp", axis=1, tiled=True),
    )
    resid_in = tokens.astype(jnp.float32)
    normed_a, hat_a, inv_a = norm_rows(resid_in, gain_a)
    first_in = normed_a.astype(jnp.bfloat16)
    projected = jnp.dot(first_in, full_qkv, preferred_element_type=jnp.float32)
    first_row = lax.axis_index("seq") * row_count
    cos_tab, sine_tab = rotary_tables(first_row, row_count, HEAD_DIM)
    head_shape = (row_count, HEADS, HEAD_DIM)
    query = (
        rotate(projected[:, :model_width].reshape(head_shape), cos_tab, sine_tab)
        .astype(jnp.bfloat16)
        .reshape(row_count, model_width)
    )
    key_local = (
        rotate(projected[:, model_width : 2 * model_width].reshape(head_shape), cos_tab, sine_tab)
        .astype(jnp.bfloat16)
        .reshape(row_count, model_width)
    )
    value_local = projected[:, 2 * model_width :].astype(jnp.bfloat16)
    key_all, value_all = (
        lax.all_gather(key_local, "seq", axis=0, tiled=True),
        lax.all_gather(value_local, "seq", axis=0, tiled=True),
    )
    attn_pairs, log_total = lax.map(
        attend, (split_pairs(query), split_pairs(key_all), split_pairs(value_all))
    )
    mixed_out = join_pairs(attn_pairs).astype(jnp.bfloat16)
    resid_mid = resid_in + jnp.dot(mixed_out, full_out, preferred_element_type=jnp.float32)
    normed_m, hat_m, inv_m = norm_rows(resid_mid, gain_m)
    second_in = normed_m.astype(jnp.bfloat16)
    rows_all = lax.all_gather(second_in, "seq", axis=0, tiled=True)
    gate_up = jnp.einsum("td,dgf->tgf", rows_all, local_in, preferred_element_type=jnp.float32)
    hidden = geglu(gate_up[:, 0], gate_up[:, 1]).astype(jnp.bfloat16)
    partial_out = jnp.dot(hidden, local_down, preferred_element_type=jnp.float32)
    mlp_out = lax.psum_scatter(
        partial_out.astype(jnp.bfloat16), "seq", scatter_dimension=0, tiled=True
    ).astype(jnp.float32)
    grad_all = lax.all_gather(grad_out, "seq", axis=0, tiled=True)
    grad_hidden = jnp.dot(grad_all, local_down.T, preferred_element_type=jnp.float32)
    grad_down = jnp.dot(hidden.T, grad_all, preferred_element_type=jnp.float32)
    _, pull_act = jax.vjp(geglu, gate_up[:, 0], gate_up[:, 1])
    grad_gate, grad_up = pull_act(grad_hidden)
    grad_both = jnp.stack([grad_gate, grad_up], 1).astype(jnp.bfloat16)
    grad_in_w = jnp.einsum("td,tgf->dgf", rows_all, grad_both, preferred_element_type=jnp.float32)
    grad_rows = jnp.einsum("tgf,dgf->td", grad_both, local_in, preferred_element_type=jnp.float32)
    grad_norm_m = lax.psum_scatter(
        grad_rows.astype(jnp.bfloat16), "seq", scatter_dimension=0, tiled=True
    ).astype(jnp.float32)
    out_block = (resid_mid + mlp_out).astype(jnp.bfloat16)
    grad_mlp_part, grad_gain_m = norm_back(grad_norm_m, gain_m, hat_m, inv_m)
    grad_mid = grad_out.astype(jnp.float32) + grad_mlp_part
    grad_attn = grad_mid.astype(jnp.bfloat16)
    grad_w_out = jnp.dot(mixed_out.T, grad_attn, preferred_element_type=jnp.float32)
    grad_mixed = jnp.dot(grad_attn, full_out.T, preferred_element_type=jnp.float32).astype(
        jnp.bfloat16
    )
    grad_query, grad_key, grad_value = lax.map(
        attend_back,
        (
            split_pairs(query),
            split_pairs(key_all),
            split_pairs(value_all),
            split_pairs(grad_mixed),
            log_total,
        ),
    )
    grad_key_own, grad_value_own = (
        lax.psum_scatter(
            join_pairs(grad_key).astype(jnp.bfloat16), "seq", scatter_dimension=0, tiled=True
        ).astype(jnp.float32),
        lax.psum_scatter(
            join_pairs(grad_value).astype(jnp.bfloat16), "seq", scatter_dimension=0, tiled=True
        ).astype(jnp.float32),
    )
    grad_query_raw = rotate_back(
        join_pairs(grad_query).reshape(head_shape), cos_tab, sine_tab
    ).reshape(row_count, model_width)
    grad_key_raw = rotate_back(grad_key_own.reshape(head_shape), cos_tab, sine_tab).reshape(
        row_count, model_width
    )
    grad_projected = jnp.concatenate([grad_query_raw, grad_key_raw, grad_value_own], -1).astype(
        jnp.bfloat16
    )
    grad_w_qkv = jnp.dot(first_in.T, grad_projected, preferred_element_type=jnp.float32)
    grad_first = jnp.dot(grad_projected, full_qkv.T, preferred_element_type=jnp.float32)
    grad_attn_part, grad_gain_a = norm_back(grad_first, gain_a, hat_a, inv_a)
    grad_tokens = (grad_mid + grad_attn_part).astype(jnp.bfloat16)
    sum_qkv, sum_out, sum_gain_a, sum_gain_m = (
        lax.psum_scatter(grad_w_qkv, ("dp", "seq"), scatter_dimension=0, tiled=True),
        lax.psum_scatter(grad_w_out, ("dp", "seq"), scatter_dimension=0, tiled=True),
        lax.psum_scatter(grad_gain_a, ("dp", "seq"), scatter_dimension=0, tiled=True),
        lax.psum_scatter(grad_gain_m, ("dp", "seq"), scatter_dimension=0, tiled=True),
    )
    sum_in, sum_down = (
        sent_and_summed(grad_in_w.astype(jnp.bfloat16), "dp", 0),
        sent_and_summed(grad_down.astype(jnp.bfloat16), "dp", 1),
    )
    return (out_block, grad_tokens, sum_qkv, sum_out, sum_gain_a, sum_gain_m, sum_in, sum_down)


def solution(mesh):
    in_specs = (
        P(("dp", "seq"), None),
        P(("dp", "seq"), None),
        P(("dp", "seq"), None),
        P(("dp", "seq")),
        P(("dp", "seq")),
        P("dp", None, "seq"),
        P("seq", "dp"),
        P(("dp", "seq"), None),
    )
    out_specs = (
        P(("dp", "seq"), None),
        P(("dp", "seq"), None),
        P(("dp", "seq"), None),
        P(("dp", "seq"), None),
        P(("dp", "seq")),
        P(("dp", "seq")),
        P("dp", None, "seq"),
        P("seq", "dp"),
    )
    return jax.shard_map(
        on_device, mesh=mesh, in_specs=in_specs, out_specs=out_specs, check_vma=False
    )
```

profile of v0, /device:TPU:0, one launch (start us, length us, event | category | flops | bytes accessed | tf_op | source)
XLA Modules:
  0.0 999.3 jit_solution(183714109443789320)
XLA Ops:
  9.7 42.0 %all-reduce.5 = (bf16[768]{0:T(1024)(128)(2,1)S(1)}, bf16[768]{0:T(1024)(128)(2,1)S(1)}) all-reduce(bf16[768]{0:T(1024)(128)(2,1)S(1)} %dynamic-update-slice, bf16[768]{0:T(1024)(128)(2,1)S(1)} %dynamic-update-slice.1), channel_id=1, replica_groups=mesh['dp'=8,'seq'=4] {'dp','seq'}, use_global_device_ids=true, to_apply=%add | all-reduce | flops 1536 | bytes 6144
  54.6 19.2 %all-gather.7.cloned.1.call-done = bf16[768,2304]{1,0:T(8,128)(2,1)} async-done(((bf16[24,2304]{1,0:T(8,128)(2,1)}), bf16[768,2304]{1,0:T(8,128)(2,1)}) %all-gather.7.cloned.1.call-update) | async-done | bytes 3538960 | tf_op jit(solution)/shard_map/all_gather | solution.py:125
  73.8 4.4 fusion.122
  87.4 4.4 add_convert_fusion.1
  96.2 47.5 %all-gather.9.cloned.1.call-done = bf16[2048,768]{1,0:T(8,128)(2,1)} async-done(((bf16[512,768]{1,0:T(8,128)(2,1)}), bf16[2048,768]{1,0:T(8,128)(2,1)}) %all-gather.9.cloned.1.call-update) | async-done | bytes 3145744 | tf_op jit(solution)/shard_map/all_gather | solution.py:156
  143.7 4.7 copy.40
  148.4 59.1 %all-gather.11.cloned.1.call-done = bf16[2048,768]{1,0:T(8,128)(2,1)} async-done(((bf16[512,768]{1,0:T(8,128)(2,1)}), bf16[2048,768]{1,0:T(8,128)(2,1)}) %all-gather.11.cloned.1.call-update) | async-done | bytes 3145744 | tf_op jit(solution)/shard_map/all_gather | solution.py:155
  207.5 3.2 copy.46
  210.7 47.2 %while.28 = (s32[]{:T(128)}, bf16[6,512,2,64]{1,3,2,0:T(8,128)(2,1)}, f32[6,2,512]{2,1,0:T(2,128)S(1)}, bf16[6,2048,2,64]{1,3,2,0:T(8,128)(2,1)}, bf16[6,512,2,6...) while((s32[]{:T(128)}, bf16[6,512,2,64]{1,3,2,0:T(8,128)(2,1)}, ...), condition=%wide.region_5.6_spmd.clone, body=%wide.region_2.5_spmd.sunk.clone | while | flops 555744256 | bytes 26642512 | solution.py:158
  210.7 2.3 multiply_reduce_fusion.8
  214.6 3.9 fusion.175
  218.6 2.3 multiply_reduce_fusion.8
  222.5 3.9 fusion.175
  226.4 2.3 multiply_reduce_fusion.8
  230.4 3.9 fusion.175
  234.3 2.3 multiply_reduce_fusion.8
  238.2 3.9 fusion.175
  242.2 2.3 multiply_reduce_fusion.8
  246.1 3.9 fusion.175
  250.1 2.3 multiply_reduce_fusion.8
  254.0 3.9 fusion.175
  257.9 5.2 all-gather.13.cloned.1.call-done
  263.1 2.6 fusion.127
  268.2 11.0 %all_gather.38 = bf16[288,768]{0,1:T(8,128)(2,1)} all-gather(bf16[288,96]{0,1:T(8,128)(2,1)S(1)} %copy.48), channel_id=1, replica_groups=mesh['dp'=8,'seq'=4] {'dp'}, dimensions={1}, use_global_device_ids=true | all-gather | bytes 497664 | tf_op jit(solution)/shard_map/all_gather | solution.py:134
  279.2 12.7 %all_gather.37 = bf16[768,2,288]{2,1,0:T(2,128)(2,1)} all-gather(bf16[96,2,288]{2,1,0:T(2,128)(2,1)S(1)} %copy-done.21), channel_id=1, replica_groups=mesh['dp'=8,'seq'=4] {'dp'}, dimensions={0}, use_global_device_ids=true | all-gather | bytes 995328 | tf_op jit(solution)/shard_map/all_gather | solution.py:133
  291.9 35.0 %all-gather.17.cloned.1.call-done = bf16[2048,768]{1,0:T(8,128)(2,1)} async-done(((bf16[512,768]{1,0:T(8,128)(2,1)}), bf16[2048,768]{1,0:T(8,128)(2,1)}) %all-gather.17.cloned.1.call-update) | async-done | bytes 3145744 | tf_op jit(solution)/shard_map/all_gather | solution.py:172
  327.0 4.6 fusion.128
  331.5 59.6 %all-gather.15.cloned.1.call-done = bf16[2048,768]{1,0:T(8,128)(2,1)} async-done(((bf16[512,768]{1,0:T(8,128)(2,1)}), bf16[2048,768]{1,0:T(8,128)(2,1)}) %all-gather.15.cloned.1.call-update) | async-done | bytes 3145744 | tf_op jit(solution)/shard_map/all_gather | solution.py:165
  391.2 4.5 fusion.53
  395.7 5.6 fusion.106
  404.5 4.2 bitcast_convert_fusion
  408.9 5.0 convolution_convert_fusion
  414.4 53.5 %reduce-scatter.9.cloned.1.call-done = bf16[512,768]{1,0:T(8,128)(2,1)} async-done(((bf16[2048,768]{1,0:T(8,128)(2,1)}), bf16[512,768]{1,0:T(8,128)(2,1)}) %reduce-scatter.9.cloned.1.call-update) | async-done | bytes 786448 | tf_op jit(solution)/shard_map/reduce_scatter | solution.py:180
  467.9 2.4 fusion.96
  470.3 60.2 %reduce-scatter.7.cloned.1.call-done = bf16[512,768]{1,0:T(8,128)(2,1)} async-done(((bf16[2048,768]{1,0:T(8,128)(2,1)}), bf16[512,768]{1,0:T(8,128)(2,1)}) %reduce-scatter.7.cloned.1.call-update) | async-done | bytes 786448 | tf_op jit(solution)/shard_map/reduce_scatter | solution.py:169
  530.5 3.7 fusion.94
  537.1 2.3 copy.50
  539.4 99.8 %while.29 = (s32[]{:T(128)}, f32[6,512,2,64]{1,3,2,0:T(8,128)}, bf16[6,2048,2,64]{1,3,2,0:T(8,128)(2,1)}, bf16[6,2048,2,64]{1,3,2,0:T(8,128)(2,1)}, bf16[6,2048,...) while((s32[]{:T(128)}, f32[6,512,2,64]{1,3,2,0:T(8,128)}, ...), condition=%wide.region_14.15_spmd.clone, body=%wide.region_12.14_spmd.sunk.clone | while | flops 1367669760 | bytes 92570776 | solution.py:191
  541.6 3.4 fusion.187
  545.0 3.4 multiply_reduce_fusion.9
  558.2 3.4 fusion.187
  561.6 3.4 multiply_reduce_fusion.9
  574.8 3.4 fusion.187
  578.2 3.4 multiply_reduce_fusion.9
  591.5 3.4 fusion.187
  594.8 3.4 multiply_reduce_fusion.9
  608.1 3.4 fusion.187
  611.5 3.4 multiply_reduce_fusion.9
  624.7 3.4 fusion.187
  628.1 3.4 multiply_reduce_fusion.9
  643.2 56.4 %reduce-scatter.11.cloned.1.call-done = bf16[512,768]{0,1:T(8,128)(2,1)} async-done(((bf16[2048,768]{0,1:T(8,128)(2,1)}), bf16[512,768]{0,1:T(8,128)(2,1)}) %reduce-scatter.11.cloned.1.call-update) | async-done | bytes 786448 | tf_op jit(solution)/shard_map/reduce_scatter | solution.py:202
  705.1 56.9 %reduce-scatter.13.cloned.1.call-done = bf16[512,768]{0,1:T(8,128)(2,1)} async-done(((bf16[2048,768]{0,1:T(8,128)(2,1)}), bf16[512,768]{0,1:T(8,128)(2,1)}) %reduce-scatter.13.cloned.1.call-update) | async-done | bytes 786448 | tf_op jit(solution)/shard_map/reduce_scatter | solution.py:205
  762.1 6.6 fusion.109
  769.9 3.7 convolution_convert_fusion.2
  776.2 4.2 all-to-all-start.1
  780.5 5.6 fusion.102
  786.0 2.4 reshape.207
  790.9 3.8 all-to-all-start
  796.6 14.9 %all-to-all-done = bf16[8,96,2,288]{1,3,2,0:T(8,128)(2,1)S(1)} async-done(((bf16[8,96,2,288]{1,3,2,0:T(8,128)(2,1)}), bf16[8,96,2,288]{1,3,2,0:T(8,128)(2,1)S(1)}, u32[]{:S(2)}, u32[]{:S(2)}) %all-to-all-start) | async-done | bytes 884768 | tf_op jit(solution)/shard_map/all_to_all | solution.py:21
  814.2 6.6 fusion.90
  820.8 39.6 %all-reduce.4 = (f32[768]{0:T(1024)S(1)}, f32[768]{0:T(1024)S(1)}) all-reduce(f32[768]{0:T(1024)S(1)} %get-tuple-element.105, f32[768]{0:T(1024)S(1)} %get-tuple-element.103), channel_id=8, replica_groups=mesh['dp'=8,'seq'=4] {'dp','seq'}, use_global_device_ids=true, to_apply=%region_22.23.clone | all-reduce | flops 1536 | bytes 12288
  861.6 2.9 fusion.89
  864.5 2.6 reduce-scatter.17.cloned.1.call-done
  867.0 125.2 %reduce-scatter.15.cloned.1.call-done = f32[24,2304]{1,0:T(8,128)} async-done(((f32[768,2304]{1,0:T(8,128)}), f32[24,2304]{1,0:T(8,128)}) %reduce-scatter.15.cloned.1.call-update) | async-done | bytes 221200 | tf_op jit(solution)/shard_map/reduce_scatter | solution.py:223
  (203 shorter events, 118.3 us)
Async XLA Ops:
  7.2 66.6 %all-gather.7.cloned.1.call-start = ((), (), s32[]{:S(2)}) async-start(), calls=%async_computation.8 | async-start | bytes 3649536 | tf_op jit(solution)/shard_map/all_gather | solution.py:125
  7.9 135.8 %all-gather.9.cloned.1.call-start = ((), (), s32[]{:S(2)}) async-start(), calls=%async_computation.9 | async-start | bytes 3932160 | tf_op jit(solution)/shard_map/all_gather | solution.py:156
  51.7 26.4 %copy-start.25 = (f32[768]{0:T(1024)}, f32[768]{0:T(1024)S(1)}, u32[]{:S(2)}) copy-start(f32[768]{0:T(1024)S(1)} %convert_element_type.123) | copy-start | bytes 9220
  53.0 25.1 %copy-start.23 = (f32[512]{0:T(512)}, f32[512]{0:T(512)S(1)}, u32[]{:S(2)}) copy-start(f32[512]{0:T(512)S(1)} %broadcast_multiply_fusion.7) | copy-start | bytes 6148
  54.5 23.6 %copy-start.27 = (f32[512]{0:T(512)}, f32[512]{0:T(512)S(1)}, u32[]{:S(2)}) copy-start(f32[512]{0:T(512)S(1)} %add_rsqrt_fusion.1) | copy-start | bytes 6148
  78.2 2.1 copy-start.5
  81.3 126.2 %all-gather.11.cloned.1.call-start = ((), (), s32[]{:S(2)}) async-start(), calls=%async_computation.10 | async-start | bytes 3932160 | tf_op jit(solution)/shard_map/all_gather | solution.py:155
  81.7 13.2 %copy-start.12 = (f32[512,64]{0,1:T(8,128)}, f32[512,64]{0,1:T(8,128)S(1)}, u32[]{:S(2)}) copy-start(f32[512,64]{0,1:T(8,128)S(1)} %get-tuple-element.167) | copy-start | bytes 393220
  81.7 13.2 %copy-start.14 = (f32[512,64]{0,1:T(8,128)}, f32[512,64]{0,1:T(8,128)S(1)}, u32[]{:S(2)}) copy-start(f32[512,64]{0,1:T(8,128)S(1)} %get-tuple-element.168) | copy-start | bytes 393220
  83.5 1.4 slice-start
  91.9 171.2 %all-gather.13.cloned.1.call-start = ((), (), s32[]{:S(2)}) async-start(), calls=%async_computation.11 | async-start | bytes 1216512 | tf_op jit(solution)/shard_map/all_gather | solution.py:126
  92.5 234.5 %all-gather.17.cloned.1.call-start = ((), (), s32[]{:S(2)}) async-start(), calls=%async_computation.14 | async-start | bytes 3932160 | tf_op jit(solution)/shard_map/all_gather | solution.py:172
  93.0 298.1 %all-gather.15.cloned.1.call-start = ((), (), s32[]{:S(2)}) async-start(), calls=%async_computation.12 | async-start | bytes 3932160 | tf_op jit(solution)/shard_map/all_gather | solution.py:165
  265.7 1.2 copy-start.1
  265.7 2.4 copy-start.22
  266.1 13.2 %copy-start.21 = (bf16[96,2,288]{2,1,0:T(2,128)(2,1)S(1)}, bf16[96,2,288]{2,1,0:T(2,128)(2,1)}, u32[]{:S(2)}) copy-start(bf16[96,2,288]{2,1,0:T(2,128)(2,1)} %param.17) | copy-start | bytes 331780
  268.0 199.8 %reduce-scatter.9.cloned.1.call-start = ((), (), s32[]{:S(2)}) async-start(), calls=%async_computation.15 | async-start | bytes 3932160 | tf_op jit(solution)/shard_map/reduce_scatter | solution.py:180
  391.2 4.5 copy-start
  401.3 2.2 copy-start.19
  401.3 3.2 copy-start.18
  403.5 1.0 copy-start.16
  408.8 121.7 %reduce-scatter.7.cloned.1.call-start = ((), (), s32[]{:S(2)}) async-start(), calls=%async_computation.13 | async-start | bytes 3932160 | tf_op jit(solution)/shard_map/reduce_scatter | solution.py:169
  413.8 285.8 %reduce-scatter.11.cloned.1.call-start = ((), (), s32[]{:S(2)}) async-start(), calls=%async_computation.16 | async-start | bytes 3932160 | tf_op jit(solution)/shard_map/reduce_scatter | solution.py:202
  530.5 4.9 copy-start.29
  534.2 1.2 copy-start.2
  550.4 2.1 copy-start.9
  554.3 1.7 copy-start.10
  567.1 2.1 copy-start.9
  571.0 1.7 copy-start.10
  583.7 2.1 copy-start.9
  587.6 1.7 copy-start.10
  600.3 2.1 copy-start.9
  604.2 1.7 copy-start.10
  616.9 2.1 copy-start.9
  620.8 1.7 copy-start.10
  633.5 2.1 copy-start.9
  637.5 1.7 copy-start.10
  639.2 1.4 copy-start.3
  639.2 1.6 copy-start.8
  639.2 122.9 %reduce-scatter.13.cloned.1.call-start = ((), (), s32[]{:S(2)}) async-start(), calls=%async_computation.17 | async-start | bytes 3932160 | tf_op jit(solution)/shard_map/reduce_scatter | solution.py:205
  639.8 227.2 %reduce-scatter.17.cloned.1.call-start = ((), (), s32[]{:S(2)}) async-start(), calls=%async_computation.19 | async-start | bytes 2433024 | tf_op jit(solution)/shard_map/reduce_scatter | solution.py:224
  643.0 56.6 %copy-start.6 = (f32[6,512,2,64]{1,3,2,0:T(8,128)S(1)}, f32[6,512,2,64]{1,3,2,0:T(8,128)}, u32[]{:S(2)}) copy-start(f32[6,512,2,64]{1,3,2,0:T(8,128)} %get-tuple-element.92) | copy-start | bytes 4718596
  643.0 56.6 %copy-start.15 = (f32[512,64]{0,1:T(8,128)S(1)}, f32[512,64]{0,1:T(8,128)}, u32[]{:S(2)}) copy-start(f32[512,64]{0,1:T(8,128)} %copy-done.14) | copy-start | bytes 393220
  643.0 349.2 %reduce-scatter.15.cloned.1.call-start = ((), (), s32[]{:S(2)}) async-start(), calls=%async_computation.18 | async-start | bytes 7299072 | tf_op jit(solution)/shard_map/reduce_scatter | solution.py:223
  701.9 1.4 copy-start.7
  701.9 1.6 copy-start.11
  701.9 1.6 copy-start.13
  703.5 58.6 %copy-start.4 = (bf16[512,768]{1,0:T(8,128)(2,1)S(1)}, bf16[512,768]{1,0:T(8,128)(2,1)}, u32[]{:S(2)}) copy-start(bf16[512,768]{1,0:T(8,128)(2,1)} %param.12) | copy-start | bytes 2359300
  703.5 58.6 %copy-start.24 = (f32[512]{0:T(512)S(1)}, f32[512]{0:T(512)}, u32[]{:S(2)}) copy-start(f32[512]{0:T(512)} %copy-done.23) | copy-start | bytes 6148
  703.5 58.6 %copy-start.26 = (f32[768]{0:T(1024)S(1)}, f32[768]{0:T(1024)}, u32[]{:S(2)}) copy-start(f32[768]{0:T(1024)} %copy-done.25) | copy-start | bytes 9220
  703.5 58.6 %copy-start.28 = (f32[512]{0:T(512)S(1)}, f32[512]{0:T(512)}, u32[]{:S(2)}) copy-start(f32[512]{0:T(512)} %copy-done.27) | copy-start | bytes 6148
  705.1 63.5 %copy-start.20 = (bf16[512,768]{0,1:T(8,128)(2,1)}, bf16[512,768]{0,1:T(8,128)(2,1)S(1)}, u32[]{:S(2)}) copy-start(bf16[512,768]{0,1:T(8,128)(2,1)S(1)} %get-tuple-element.163) | copy-start | bytes 2359300
  768.7 1.3 copy-start.17
  776.2 14.7 %all-to-all-start.1 = ((bf16[8,288,96]{2,1,0:T(8,128)(2,1)}), bf16[8,288,96]{2,1,0:T(8,128)(2,1)}, u32[]{:S(2)}, u32[]{:S(2)}) async-start(bf16[8,288,96]{2,1,0:T(8,128)(2,1)} %bitcast.231), calls=%async_computation.7 | async-start | bytes 1179648 | tf_op jit(solution)/shard_map/all_to_all | solution.py:21
  790.9 20.5 %all-to-all-start = ((bf16[8,96,2,288]{1,3,2,0:T(8,128)(2,1)}), bf16[8,96,2,288]{1,3,2,0:T(8,128)(2,1)S(1)}, u32[]{:S(2)}, u32[]{:S(2)}) async-start(bf16[8,96,2,288]{1,3,2,0:T(8,128)(2,1)} %copy.51), calls=%async_computation.6 | async-start | bytes 2359296 | tf_op jit(solution)/shard_map/all_to_all | solution.py:21
Sparse Core Ops, SparseCore 0:
  10.8 62.9 all-gather.6
  81.4 62.2 all-gather.8
  145.3 62.1 all-gather.10
  210.1 52.8 all-gather.12
  264.5 62.4 all-gather.16
  329.0 62.1 all-gather.14
  408.9 58.8 reduce-scatter.8
  470.2 60.2 reduce-scatter.6
  639.3 60.2 reduce-scatter.10
  701.8 60.2 reduce-scatter.12
  768.0 99.0 reduce-scatter.16
  874.1 118.1 reduce-scatter.14
where the time goes:
time: 1010 us; the launch traced here: 999 us
  waiting for transfers between devices  599 us (59%)
  matrix products  166 us (16%)
  blocking collectives  105 us (10%)
  other arithmetic  57.6 us (6%)
  local copies, waits for them, and re-layouts  46.9 us (5%)
  between operations  14.9 us (1%)
    reduce_scatter x1, waiting for transfers between devices, on_device(): lax.psum_scatter(grad_w_qkv, ('dp', 'seq'), scatter_dimension=0, tiled=True)  125 us
    unnamed x2, blocking collectives  81.7 us
    reduce_scatter x1, waiting for transfers between devices, on_device(): lax.psum_scatter(partial_out.astype(jnp.bfloat16), 'seq', scatter_dimensi...  60.2 us
    all_gather x1, waiting for transfers between devices, on_device(): rows_all = lax.all_gather(second_in, 'seq', axis=0, tiled=True)  59.6 us
    all_gather x1, waiting for transfers between devices, on_device(): lax.all_gather(key_local, 'seq', axis=0, tiled=True)  59.1 us
    reduce_scatter x1, waiting for transfers between devices, on_device(): lax.psum_scatter(join_pairs(grad_value).astype(jnp.bfloat16), 'seq', scat...  56.9 us
    reduce_scatter x1, waiting for transfers between devices, on_device(): lax.psum_scatter(join_pairs(grad_key).astype(jnp.bfloat16), 'seq', scatte...  56.4 us
    reduce_scatter x1, waiting for transfers between devices, on_device(): lax.psum_scatter(grad_rows.astype(jnp.bfloat16), 'seq', scatter_dimension...  53.5 us
  transfers between devices with their start and end apart: 14, of which 14 were waited for; matrix products, arithmetic and copies ran while one was open for 13% of the time, Pallas kernels for 0%

commit v1 on v0

v1 whole, which is shorter than its diff:
```python
import functools
import math

import jax
import jax.numpy as jnp
import numpy as np
from jax import lax
from jax.experimental import pallas as pl
from jax.experimental.pallas import tpu as pltpu
from jax.sharding import PartitionSpec as P

HEADS = 12
HEAD_DIM = 64
NORM_EPS = 1e-05
ROPE_THETA = 160000.0

F32 = jnp.float32
BF = jnp.bfloat16
MESH = pl.DeviceIdType.MESH
NT = (((1,), (1,)), ((), ()))
NN = (((1,), (0,)), ((), ()))
TN = (((0,), (0,)), ((), ()))

WIDTH = 768
PAIRS = HEADS // 2
UNITS = 1152
GROUPS = 8
LINE = 4
BAND = WIDTH // GROUPS
SLIVER = BAND // LINE
SHARE = UNITS // LINE
MAIN = 256
REST = SHARE - MAIN
LOG2E = math.log2(math.e)
SCALE = HEAD_DIM**-0.5


def dot(a, b, dims):
    return lax.dot_general(a, b, dims, preferred_element_type=F32)


def lanes_of(tile, width=128):
    return pl.ds(pl.multiple_of(tile * width, width), width)


def lane_iota():
    return lax.broadcasted_iota(jnp.int32, (1, 128), 1)


def swap_halves(u):
    low = lax.rem(lane_iota(), 64) < 32
    return jnp.where(low, pltpu.roll(u, 96, 1), pltpu.roll(u, 32, 1))


def rope(u, cos, sine):
    return u * cos + swap_halves(u) * sine


def rope_back(u, cos, sine):
    return u * cos - swap_halves(u) * sine


def rope_tables(rows):
    position = np.arange(rows, dtype=np.float32)
    half = HEAD_DIM // 2
    freq = (ROPE_THETA ** (-np.arange(half) * 2.0 / HEAD_DIM)).astype(np.float32)
    angle = (position[:, None] * freq[None, :]).astype(np.float64)
    cos, sine = np.cos(angle), np.sin(angle)
    cos = np.concatenate([cos] * 4, 1).astype(np.float32)
    sine = np.concatenate([-sine, sine] * 2, 1).astype(np.float32)
    return cos, sine


def normed(x):
    centred = x - jnp.mean(x, -1, keepdims=True)
    inv = lax.rsqrt(jnp.mean(centred * centred, -1, keepdims=True) + NORM_EPS)
    return centred * inv, inv


def norm_back(dy, gain, hat, inv):
    d = dy * gain
    return inv * (d - jnp.mean(d, -1, keepdims=True) - hat * jnp.mean(d * hat, -1, keepdims=True))


def chunk_at(z, t, nz):
    both = jnp.minimum(z, nz - 1 - z)
    near = jnp.where(lax.rem(t, 2) == 1, z - (t + 1) // 2, z + (t + 1) // 2)
    far = jnp.where(z < nz - 1 - z, z + t - both, z - t + both)
    return jnp.where(t <= 2 * both, near, far)


def remote(src, dst, send, recv, device):
    return pltpu.make_async_remote_copy(src, dst, send, recv, device_id=device, device_id_type=MESH)


def greet(z, nz, dp, masks):
    bar = pltpu.get_barrier_semaphore()
    for o in range(1, nz):
        pl.semaphore_signal(bar, inc=1, device_id={"seq": lax.rem(z + o, nz)}, device_id_type=MESH)
    for m in masks:
        pl.semaphore_signal(bar, inc=1, device_id={"dp": dp ^ m}, device_id_type=MESH)
    pl.semaphore_wait(bar, nz - 1 + len(masks))


class Gather:
    COPIES = 9

    def __init__(self, src, out, cut, nz, masks, send, recv):
        self.src, self.out, self.cut, self.nz, self.masks = src, out, cut, nz, masks
        self.send, self.recv = send, recv
        self.dp, self.z = lax.axis_index("dp"), lax.axis_index("seq")
        self.started = []

    @staticmethod
    def sems(nz):
        return Gather.COPIES * nz + nz

    def key(self, o, k):
        return o * self.COPIES + k

    def copy(self, src, dst, device, k):
        return remote(src, dst, self.send.at[k], self.recv.at[k], device)

    def begin(self, src, dst, device, k):
        c = self.copy(src, dst, device, k)
        c.start()
        self.started.append(c)

    def arrived(self, ref, k):
        self.copy(ref, ref, {"dp": self.dp ^ self.masks[0]}, k).wait_recv()

    def slot(self, o):
        return lax.rem(self.z + self.nz - o, self.nz)

    def part(self, ref, p):
        if p is None:
            return ref
        width = self.out.shape[-1]
        return ref.at[:, pl.ds(0, self.cut)] if p == 0 else ref.at[:, pl.ds(self.cut, width - self.cut)]

    def along(self):
        for o in range(1, self.nz):
            k = self.COPIES * self.nz + o
            self.begin(self.src, self.out.at[self.dp, self.z], {"seq": lax.rem(self.z + o, self.nz)}, k)

    def forward(self, src, d, s, mask, k, p=None):
        dst = self.out.at[d, s]
        self.begin(self.part(src, p), self.part(dst, p), {"dp": self.dp ^ mask}, k)

    def first(self, o):
        my, mx, mc = self.masks
        s = self.slot(o)
        src = self.src
        if o:
            src = self.out.at[self.dp, s]
            self.arrived(src, self.COPIES * self.nz + o)
        self.forward(src, self.dp, s, my, self.key(o, 0))
        self.forward(src, self.dp, s, mx, self.key(o, 1))
        self.forward(src, self.dp, s, mc, self.key(o, 2))

    def second(self, o):
        my, mx, mc = self.masks
        s = self.slot(o)
        for m, k, k2, kc, p, m2 in ((my, 0, 3, 4, 0, mx), (mx, 1, 5, 6, 1, my)):
            ref = self.out.at[self.dp ^ m, s]
            self.arrived(ref, self.key(o, k))
            self.forward(ref, self.dp ^ m, s, m2, self.key(o, k2), p)
            self.forward(ref, self.dp ^ m, s, mc, self.key(o, kc))

    def third(self, o):
        my, mx, mc = self.masks
        s = self.slot(o)
        d = self.dp ^ my ^ mx
        for p, k, kc in ((0, 3, 7), (1, 5, 8)):
            ref = self.out.at[d, s]
            self.arrived(self.part(ref, p), self.key(o, k))
            self.forward(ref, d, s, mc, self.key(o, kc), p)

    def finish(self, o):
        my, mx, mc = self.masks
        s = self.slot(o)
        for k, d in ((2, mc), (4, mc ^ my), (6, mc ^ mx)):
            self.arrived(self.out.at[self.dp ^ d, s], self.key(o, k))
        for k, p in ((7, 0), (8, 1)):
            self.arrived(self.part(self.out.at[self.dp ^ mc ^ my ^ mx, s], p), self.key(o, k))

    def done(self):
        for c in self.started:
            c.wait_send()


def half_lanes(width):
    return (width // 256) * 128


def front_kernel(nz, masks, rows, *refs):
    fused = masks is not None
    if fused:
        (tok, pq, po, pm, cos, sine, mixed, lse, query, keys, values, firsts, wqkv, gain, po_all, pm_all, tok_all, pq_all,
         gcol, acc, top, total, tsend, trecv, qs, qr, os_, or_, ms, mr, loc) = refs
    else:
        (tok, pq_all, cos, sine, mixed, lse, query, keys, values, firsts, wqkv, gain, tok_all,
         gcol, acc, top, total, tsend, trecv, loc) = refs
    dp, z = lax.axis_index("dp"), lax.axis_index("seq")

    own = pltpu.make_async_copy(tok, tok_all.at[z], loc.at[0])
    own.start()
    if fused:
        locals_ = []
        for i, (src, out) in enumerate(((pq, pq_all), (po, po_all), (pm, pm_all))):
            c = pltpu.make_async_copy(src, out.at[dp, z], loc.at[1 + i])
            c.start()
            locals_.append(c)
        greet(z, nz, dp, masks)
        packs = [
            Gather(pq, pq_all, half_lanes(pq.shape[-1]), nz, masks, qs, qr),
            Gather(po, po_all, half_lanes(po.shape[-1]), nz, masks, os_, or_),
            Gather(pm, pm_all, half_lanes(pm.shape[-1]), nz, masks, ms, mr),
        ]
        first, *later = packs
        first.along()
        first.first(0)
    else:
        bar = pltpu.get_barrier_semaphore()
        for o in range(1, nz):
            pl.semaphore_signal(bar, inc=1, device_id={"seq": lax.rem(z + o, nz)}, device_id_type=MESH)
        pl.semaphore_wait(bar, nz - 1)

    def hop(src, c, left):
        to = z - 1 if left else z + 1
        k = nz if left else c
        if src is None:
            src = tok_all.at[c]
            k = c
        return remote(src, tok_all.at[c], tsend.at[k], trecv.at[c], {"seq": to})

    @pl.when(z + 1 < nz)
    def _():
        hop(tok, z, False).start()

    @pl.when(z > 0)
    def _():
        hop(tok, z, True).start()

    if fused:
        for g in later:
            g.along()
        first.second(0)
        for o in range(1, nz):
            first.first(o)
        for o in range(1, nz):
            first.second(o)
        for o in range(nz):
            first.third(o)
        for g in later:
            for o in range(nz):
                g.first(o)
        for o in range(nz):
            first.finish(o)
        for c in locals_:
            c.wait()
    own.wait()

    half = 1152

    def build(g, _):
        slabs = [pq_all[g, s].astype(F32) for s in range(LINE)]
        band = pl.ds(pl.multiple_of(g * BAND, BAND), BAND)
        wqkv[band, :half] = jnp.concatenate([x[:SLIVER, :half] for x in slabs], 0).astype(BF)
        wqkv[band, half:] = jnp.concatenate([x[SLIVER:, :half] for x in slabs], 0).astype(BF)
        gcol[band, :] = jnp.concatenate([x[:SLIVER, half:] for x in slabs], 0)
        return 0

    lax.fori_loop(0, GROUPS, build, 0)
    gain[...] = gcol[...].T[:8]

    def norm_chunk(c):
        def block(i, _):
            at = pl.ds(pl.multiple_of(i * 64, 64), 64)
            hat, _ = normed(tok_all[c, at, :].astype(F32))
            firsts[c, at, :] = (hat * gain[0:1, :]).astype(BF)
            return 0

        lax.fori_loop(0, rows // 64, block, 0)

    def project(c, j, base):
        return dot(firsts[c], wqkv[:, base + 256 * j : base + 256 * j + 256], NN)

    norm_chunk(z)
    for j in range(3):
        u = project(z, j, 0)
        for i in range(2):
            tile = rope(u[:, 128 * i : 128 * i + 128], cos[z], sine[z])
            query[:, 256 * j + 128 * i : 256 * j + 128 * i + 128] = (tile * (SCALE * LOG2E)).astype(BF)
    acc[...] = jnp.zeros_like(acc)
    total[...] = jnp.zeros_like(total)
    top[...] = jnp.full_like(top, -1e30)

    def visit(t, _):
        c = chunk_at(z, t, nz)

        @pl.when(t > 0)
        def _():
            remote(tok_all.at[c], tok_all.at[c], tsend.at[c], trecv.at[c], {"seq": lax.rem(z + 1, nz)}).wait_recv()

            @pl.when((c < z) & (z + 1 < nz))
            def _():
                hop(None, c, False).start()

            @pl.when((c > z) & (z > 0))
            def _():
                hop(None, c, True).start()

            norm_chunk(c)

        for j in range(3):
            u = project(c, j, WIDTH)
            for i in range(2):
                at = 256 * j + 128 * i
                keys[c, :, at : at + 128] = rope(u[:, 128 * i : 128 * i + 128], cos[c], sine[c]).astype(BF)
            values[c, :, 256 * j : 256 * j + 256] = project(c, j, 2 * WIDTH).astype(BF)

        def pair(hp, _):
            q, k, v = query[:, lanes_of(hp)], keys[c, :, lanes_of(hp)], values[c, :, lanes_of(hp)]
            for h in range(2):
                mask = (lane_iota() < 64) if h == 0 else (lane_iota() >= 64)
                s = dot(k, jnp.where(mask, q, jnp.zeros_like(q)), NT)
                at = pl.ds(hp * 2 + h, 1)
                old = top[at, :]
                new = jnp.maximum(old, jnp.max(s, 0, keepdims=True))
                p = jnp.exp2(s - new)
                fade = jnp.exp2(old - new)
                top[at, :] = new
                total[at, :] = total[at, :] * fade + jnp.sum(p, 0, keepdims=True)
                band = pl.ds(pl.multiple_of(hp * 128 + h * 64, 64), 64)
                acc[band, :] = acc[band, :] * fade + dot(v[:, h * 64 : h * 64 + 64], p.astype(BF), TN)
            return 0

        lax.fori_loop(0, PAIRS, pair, 0)
        return 0

    lax.fori_loop(0, nz, visit, 0)

    for hp in range(PAIRS):
        parts = [
            acc[128 * hp + 64 * h : 128 * hp + 64 * h + 64, :] / total[2 * hp + h : 2 * hp + h + 1, :] for h in range(2)
        ]
        mixed[:, 128 * hp : 128 * hp + 128] = jnp.concatenate(parts, 0).T.astype(BF)
    lse[...] = top[...] + jnp.log(jnp.maximum(total[...], 1e-30)) * LOG2E

    if fused:
        for g in later:
            for o in range(nz):
                g.second(o)
        for g in later:
            for o in range(nz):
                g.third(o)
        for g in later:
            for o in range(nz):
                g.finish(o)
        for g in packs:
            g.done()

    @pl.when(z + 1 < nz)
    def _():
        hop(tok, z, False).wait_send()

    @pl.when(z > 0)
    def _():
        hop(tok, z, True).wait_send()

    for t in range(1, nz):
        c = chunk_at(z, t, nz)

        @pl.when(((c < z) & (z + 1 < nz)) | ((c > z) & (z > 0)))
        def _(c=c):
            hop(None, c, False).wait_send()


def front(tok, packs, cos, sine, nz, masks):
    rows = tok.shape[0]
    fused = masks is not None
    vmem, anyspace = pl.BlockSpec(memory_space=pltpu.VMEM), pl.BlockSpec(memory_space=pl.ANY)
    shape = jax.ShapeDtypeStruct
    outs = [
        shape((rows, WIDTH), BF),
        shape((16, rows), F32),
        shape((rows, WIDTH), BF),
        shape((nz, rows, WIDTH), BF),
        shape((nz, rows, WIDTH), BF),
        shape((nz, rows, WIDTH), BF),
        shape((WIDTH, 3 * WIDTH), BF),
        shape((8, WIDTH), F32),
    ]
    out_specs = [vmem] * 8
    scratch = [pltpu.VMEM((nz, rows, WIDTH), BF)]
    if fused:
        pq, po, pm = packs
        outs += [shape((GROUPS, nz) + po.shape, BF), shape((GROUPS, nz) + pm.shape, BF)]
        out_specs += [anyspace] * 2
        in_specs = [anyspace] * 4 + [vmem] * 2
        scratch += [pltpu.VMEM((GROUPS, nz) + pq.shape, BF)]
    else:
        in_specs = [anyspace] + [vmem] * 3
    scratch += [
        pltpu.VMEM((WIDTH, 128), F32),
        pltpu.VMEM((WIDTH, rows), F32),
        pltpu.VMEM((16, rows), F32),
        pltpu.VMEM((16, rows), F32),
        pltpu.SemaphoreType.DMA((nz + 1,)),
        pltpu.SemaphoreType.DMA((nz,)),
    ]
    if fused:
        scratch += [pltpu.SemaphoreType.DMA((Gather.sems(nz),)) for _ in range(6)]
    scratch += [pltpu.SemaphoreType.DMA((4,))]
    return pl.pallas_call(
        functools.partial(front_kernel, nz, masks, rows),
        out_shape=outs,
        in_specs=in_specs,
        out_specs=out_specs,
        scratch_shapes=scratch,
        compiler_params=pltpu.CompilerParams(collective_id=0, has_side_effects=True, vmem_limit_bytes=58 << 20),
        cost_estimate=pl.CostEstimate(flops=14_000_000_000, bytes_accessed=40_000_000, transcendentals=13_000_000),
        name="front",
    )(tok, *packs, cos, sine)


def middle_kernel(rows, tok, mixed, gout, po_all, pm_all, out, gmid, gmixed, delta, po_g, pm_g,
                  wout, wg, wu, wd, gcol, gain, resid, hat, inv, second, hidden, ggate, gup, gsec, gattn, dwout):
    lane = lane_iota()

    def build(g, _):
        band = pl.ds(pl.multiple_of(g * BAND, BAND), BAND)
        slabs = [po_all[g, s].astype(F32) for s in range(LINE)]
        wout[band, :384] = jnp.concatenate([x[:SLIVER, :384] for x in slabs], 0).astype(BF)
        wout[band, 384:] = jnp.concatenate([x[SLIVER:, :384] for x in slabs], 0).astype(BF)
        gcol[band, :] = jnp.concatenate([x[:SLIVER, 384:] for x in slabs], 0)
        for i, w in enumerate((wg, wu, wd)):
            tail = jnp.zeros((BAND, 128), F32)
            for s in range(LINE):
                w[band, MAIN * s : MAIN * s + MAIN] = pm_all[g, s, :, MAIN * i : MAIN * i + MAIN]
                rest = pm_all[g, s, :, 3 * MAIN :].astype(F32)
                turn = (REST * (s - i)) % 128
                rest = pltpu.roll(rest, turn, 1) if turn else rest
                tail = jnp.where((lane >= REST * s) & (lane < REST * (s + 1)), rest, tail)
            w[band, MAIN * LINE :] = tail.astype(BF)
        return 0

    lax.fori_loop(0, GROUPS, build, 0)
    gain[...] = gcol[...].T[:8]

    for j in range(3):
        at = slice(256 * j, 256 * j + 256)
        resid[:, at] = tok[:, at].astype(F32) + dot(mixed[...], wout[:, at], NN)

    def norm_block(i, _):
        at = pl.ds(pl.multiple_of(i * 64, 64), 64)
        h, r = normed(resid[at, :])
        hat[at, :] = h
        inv[at, :] = jnp.broadcast_to(r, (64, 128))
        second[at, :] = (h * gain[0:1, :]).astype(BF)
        return 0

    lax.fori_loop(0, rows // 64, norm_block, 0)

    def units(start, width):
        at = pl.ds(start, width)
        gate, up, gh = dot(second[...], wg[:, at], NN), dot(second[...], wu[:, at], NN), dot(gout[...], wd[:, at], NN)
        cdf = 0.5 + 0.5 * lax.erf(gate * math.sqrt(0.5))
        pdf = jnp.exp2(gate * gate * (-0.5 * LOG2E)) * (1.0 / math.sqrt(2.0 * math.pi))
        act = gate * cdf
        hidden[:, at] = (act * up).astype(BF)
        gup[:, at] = (gh * act).astype(BF)
        ggate[:, at] = (gh * up * (cdf + gate * pdf)).astype(BF)

    def unit_block(i, _):
        units(pl.multiple_of(i * 128, 128), 128)
        return 0

    lax.fori_loop(0, UNITS // 128, unit_block, 0)

    for j in range(3):
        at = slice(256 * j, 256 * j + 256)
        out[:, at] = (resid[:, at] + dot(hidden[...], wd[at, :], NT)).astype(BF)
        gsec[:, at] = dot(ggate[...], wg[at, :], NT) + dot(gup[...], wu[at, :], NT)

    def back_block(i, dgain):
        at = pl.ds(pl.multiple_of(i * 64, 64), 64)
        dy, h = gsec[at, :], hat[at, :]
        gm = gout[at, :].astype(F32) + norm_back(dy, gain[0:1, :], h, inv[at, 0:1])
        gmid[at, :] = gm
        gattn[at, :] = gm.astype(BF)
        return dgain + jnp.sum(dy * h, 0, keepdims=True)

    dgain = lax.fori_loop(0, rows // 64, back_block, jnp.zeros((1, WIDTH), F32))

    heads = lax.broadcasted_iota(jnp.int32, (16, 256), 0)
    for j in range(3):
        at = slice(256 * j, 256 * j + 256)
        gmx = dot(gattn[...], wout[at, :], NT).astype(BF)
        gmixed[:, at] = gmx
        prod = gmx.astype(F32) * mixed[:, at].astype(F32)
        high = prod.astype(BF)
        low = (prod - high.astype(F32)).astype(BF)
        pick = ((lax.broadcasted_iota(jnp.int32, (16, 256), 1) + 256 * j) // HEAD_DIM == heads).astype(BF)
        part = dot(pick, high, NT) + dot(pick, low, NT)
        delta[...] = part if j == 0 else delta[...] + part

    for j in range(2):
        at = slice(384 * j, 384 * j + 384)
        dwout[at, :] = dot(mixed[:, at], gattn[...], TN)
    row = lax.broadcasted_iota(jnp.int32, (128, WIDTH), 0)
    gcol[...] = jnp.where(row == 0, dgain, 0.0).T

    def pack_out(g, _):
        for s in range(LINE):
            at = pl.ds(pl.multiple_of(g * BAND + s * SLIVER, 8), SLIVER)
            x, c = dwout[at, :], gcol[at, :]
            po_g[g, s, :, :384] = jnp.concatenate([x[:, :384], x[:, 384:]], 0).astype(BF)
            po_g[g, s, :, 384:] = jnp.concatenate([c, jnp.zeros_like(c)], 0).astype(BF)
        return 0

    lax.fori_loop(0, GROUPS, pack_out, 0)

    for j in range(2):
        at = slice(384 * j, 384 * j + 384)
        tails = []
        for i, (a, b) in enumerate(((second, ggate), (second, gup), (gout, hidden))):
            for s in range(LINE):
                x = dot(a[:, at], b[:, MAIN * s : MAIN * s + MAIN], TN).astype(BF)
                for g in range(4):
                    pm_g[4 * j + g, s, :, MAIN * i : MAIN * i + MAIN] = x[BAND * g : BAND * g + BAND]
            tails.append(dot(a[:, at], b[:, MAIN * LINE :], TN))
        for s in range(LINE):
            y = jnp.zeros((384, 128), F32)
            for i, tail in enumerate(tails):
                turn = (REST * (i - s)) % 128
                tail = pltpu.roll(tail, turn, 1) if turn else tail
                y = jnp.where((lane >= REST * i) & (lane < REST * (i + 1)), tail, y)
            y = y.astype(BF)
            for g in range(4):
                pm_g[4 * j + g, s, :, 3 * MAIN :] = y[BAND * g : BAND * g + BAND]


def middle(tok, mixed, gout, po_all, pm_all):
    rows = tok.shape[0]
    shape, vm = jax.ShapeDtypeStruct, pltpu.VMEM
    vmem = pl.BlockSpec(memory_space=pltpu.VMEM)
    return pl.pallas_call(
        functools.partial(middle_kernel, rows),
        out_shape=[
            shape((rows, WIDTH), BF),
            shape((rows, WIDTH), F32),
            shape((rows, WIDTH), BF),
            shape((16, rows), F32),
            shape(po_all.shape, BF),
            shape(pm_all.shape, BF),
        ],
        in_specs=[vmem] * 5,
        out_specs=[vmem] * 6,
        scratch_shapes=[
            vm((WIDTH, WIDTH), BF),
            vm((WIDTH, UNITS), BF),
            vm((WIDTH, UNITS), BF),
            vm((WIDTH, UNITS), BF),
            vm((WIDTH, 128), F32),
            vm((8, WIDTH), F32),
            vm((rows, WIDTH), F32),
            vm((rows, WIDTH), F32),
            vm((rows, 128), F32),
            vm((rows, WIDTH), BF),
            vm((rows, UNITS), BF),
            vm((rows, UNITS), BF),
            vm((rows, UNITS), BF),
            vm((rows, WIDTH), F32),
            vm((rows, WIDTH), BF),
            vm((WIDTH, WIDTH), F32),
        ],
        compiler_params=pltpu.CompilerParams(vmem_limit_bytes=58 << 20),
        cost_estimate=pl.CostEstimate(flops=11_000_000_000, bytes_accessed=25_000_000, transcendentals=1_200_000),
        name="middle",
    )(tok, mixed, gout, po_all, pm_all)


def back_kernel(nz, rows, tok, gmid, query, keys, values, firsts, wqkv, gain, gmixed, lse, delta, cos, sine,
                gtok, pq_g, dq, dkv, dx, dw, posted, landed, gcol, send, recv):
    z = lax.axis_index("seq")
    bar = pltpu.get_barrier_semaphore()
    for o in range(1, nz):
        pl.semaphore_signal(bar, inc=1, device_id={"seq": lax.rem(z + o, nz)}, device_id_type=MESH)
    pl.semaphore_wait(bar, nz - 1)
    dq[...] = jnp.zeros_like(dq)
    dw[...] = jnp.zeros_like(dw)

    def post(c):
        k = lax.rem(z - c + nz, nz) - 1
        return remote(posted.at[k], landed.at[k], send.at[k], recv.at[k], {"seq": c})

    def visit(t, _):
        c = chunk_at(z, nz - 1 - t, nz)

        def pair(hp, _):
            at = lanes_of(hp)
            q, g, k, v = query[:, at], gmixed[:, at], keys[c, :, at], values[c, :, at]
            dk = dv = None
            for h in range(2):
                mask = (lane_iota() < 64) if h == 0 else (lane_iota() >= 64)
                qh, gh = jnp.where(mask, q, jnp.zeros_like(q)), jnp.where(mask, g, jnp.zeros_like(g))
                head = pl.ds(hp * 2 + h, 1)
                p = jnp.exp2(dot(k, qh, NT) - lse[head, :])
                ds = (p * (dot(v, gh, NT) - delta[head, :])).astype(BF)
                a = dot(p.astype(BF), gh, NN)
                dv = a if dv is None else dv + a
                a = dot(ds, qh, NN)
                dk = a if dk is None else dk + a
                band = pl.ds(pl.multiple_of(hp * 128 + h * 64, 64), 64)
                dq[band, :] += dot(k[:, h * 64 : h * 64 + 64], ds, TN)
            dkv[:, at] = rope_back(dk * (1.0 / LOG2E), cos[c], sine[c]).astype(BF)
            dkv[:, lanes_of(hp + PAIRS)] = dv.astype(BF)
            return 0

        lax.fori_loop(0, PAIRS, pair, 0)

        for j in range(3):
            at = slice(256 * j, 256 * j + 256)
            x = dot(dkv[...], wqkv[at, WIDTH:], NT)
            dx[:, at] = x

        @pl.when(c != z)
        def _():
            k = lax.rem(z - c + nz, nz) - 1
            posted[k] = dx[...].astype(BF)
            post(c).start()

        def weigh(i, _):
            at, to = lanes_of(i, 256), lanes_of(i + 3, 256)
            for j in range(2):
                r = slice(384 * j, 384 * j + 384)
                dw[r, to] += dot(firsts[c, :, r], dkv[:, at], TN)
            return 0

        lax.fori_loop(0, 6, weigh, 0)
        return 0

    lax.fori_loop(0, nz, visit, 0)

    for hp in range(PAIRS):
        at = slice(128 * hp, 128 * hp + 128)
        u = dq[at, :].T * SCALE
        dkv[:, at] = rope_back(u, cos[z], sine[z]).astype(BF)
    for j in range(3):
        at = slice(256 * j, 256 * j + 256)
        dx[:, at] += dot(dkv[:, :WIDTH], wqkv[at, :WIDTH], NT)
        for i in range(2):
            r = slice(384 * i, 384 * i + 384)
            dw[r, at] = dot(firsts[z, :, r], dkv[:, at], TN)

    for o in range(1, nz):
        post(lax.rem(z + nz - o, nz)).wait_recv()

    def norm_block(i, dgain):
        at = pl.ds(pl.multiple_of(i * 64, 64), 64)
        dy = dx[at, :]
        for k in range(nz - 1):
            dy = dy + landed[k, at, :].astype(F32)
        h, r = normed(tok[at, :].astype(F32))
        gtok[at, :] = (gmid[at, :] + norm_back(dy, gain[0:1, :], h, r)).astype(BF)
        return dgain + jnp.sum(dy * h, 0, keepdims=True)

    dgain = lax.fori_loop(0, rows // 64, norm_block, jnp.zeros((1, WIDTH), F32))
    row = lax.broadcasted_iota(jnp.int32, (128, WIDTH), 0)
    gcol[...] = jnp.where(row == 0, dgain, 0.0).T

    def pack(g, _):
        for s in range(LINE):
            at = pl.ds(pl.multiple_of(g * BAND + s * SLIVER, 8), SLIVER)
            x, c = dw[at, :], gcol[at, :]
            pq_g[g, s, :, :1152] = jnp.concatenate([x[:, :1152], x[:, 1152:]], 0).astype(BF)
            pq_g[g, s, :, 1152:] = jnp.concatenate([c, jnp.zeros_like(c)], 0).astype(BF)
        return 0

    lax.fori_loop(0, GROUPS, pack, 0)
    for o in range(1, nz):
        post(lax.rem(z + nz - o, nz)).wait_send()


def back(tok, gmid, query, keys, values, firsts, wqkv, gain, gmixed, lse, delta, cos, sine, nz):
    rows = tok.shape[0]
    shape, vm = jax.ShapeDtypeStruct, pltpu.VMEM
    vmem = pl.BlockSpec(memory_space=pltpu.VMEM)
    return pl.pallas_call(
        functools.partial(back_kernel, nz, rows),
        out_shape=[shape((rows, WIDTH), BF), shape((GROUPS, LINE, 2 * SLIVER, 1280), BF)],
        in_specs=[vmem] * 13,
        out_specs=[vmem] * 2,
        scratch_shapes=[
            vm((WIDTH, rows), F32),
            vm((rows, 2 * WIDTH), BF),
            vm((rows, WIDTH), F32),
            vm((WIDTH, 3 * WIDTH), F32),
            vm((nz - 1, rows, WIDTH), BF),
            vm((nz - 1, rows, WIDTH), BF),
            vm((WIDTH, 128), F32),
            pltpu.SemaphoreType.DMA((nz - 1,)),
            pltpu.SemaphoreType.DMA((nz - 1,)),
        ],
        compiler_params=pltpu.CompilerParams(collective_id=1, has_side_effects=True, vmem_limit_bytes=58 << 20),
        cost_estimate=pl.CostEstimate(flops=24_000_000_000, bytes_accessed=40_000_000, transcendentals=13_000_000),
        name="back",
    )(tok, gmid, query, keys, values, firsts, wqkv, gain, gmixed, lse, delta, cos, sine)


class Reduce:
    COPIES = 10

    def __init__(self, src, total, cut, nz, masks, bufs, send, recv, loc):
        self.src, self.total, self.cut, self.nz, self.masks = src, total, cut, nz, masks
        self.mine, self.near, self.side0, self.side1, self.far = bufs
        self.send, self.recv, self.loc = send, recv, loc
        self.dp, self.z = lax.axis_index("dp"), lax.axis_index("seq")
        my, mx, mc = masks
        self.turns = (0, my, mx, my ^ mx)
        self.started = []

    @staticmethod
    def scratch(shape, cut, nz):
        r, c = shape
        return [
            pltpu.VMEM((4, nz, r, c), BF),
            pltpu.VMEM((4, nz, r, c), BF),
            pltpu.VMEM((3, nz, r, cut), BF),
            pltpu.VMEM((3, nz, r, c - cut), BF),
            pltpu.VMEM((nz - 1, r, c), BF),
        ], [
            pltpu.SemaphoreType.DMA((Reduce.COPIES * nz + nz,)),
            pltpu.SemaphoreType.DMA((Reduce.COPIES * nz + nz,)),
            pltpu.SemaphoreType.DMA((4 * nz,)),
        ]

    def begin(self, src, dst, device, k):
        c = remote(src, dst, self.send.at[k], self.recv.at[k], device)
        c.start()
        self.started.append(c)

    def arrived(self, ref, k):
        remote(ref, ref, self.send.at[k], self.recv.at[k], {"dp": self.dp ^ self.masks[2]}).wait_recv()

    def seat(self, o):
        return lax.rem(self.z + o, self.nz)

    def local(self, i, o):
        s = self.seat(o)
        return pltpu.make_async_copy(self.src.at[self.dp ^ self.turns[i], s], self.mine.at[i, s], self.loc.at[4 * o + i])

    def zero(self, o):
        s, mc = self.seat(o), self.masks[2]
        for i in (3, 1, 2, 0):
            self.local(i, o).start()
            self.begin(self.src.at[self.dp ^ mc ^ self.turns[i], s], self.near.at[i, s], {"dp": self.dp ^ mc}, self.COPIES * o + i)

    def add(self, ref, other):
        ref[...] = (ref[...].astype(F32) + other[...].astype(F32)).astype(BF)

    def p0(self, i, s):
        return self.mine.at[i, s, :, pl.ds(0, self.cut)]

    def p1(self, i, s):
        return self.mine.at[i, s, :, pl.ds(self.cut, self.mine.shape[-1] - self.cut)]

    def one(self, o):
        my, mx, _ = self.masks
        s, k = self.seat(o), self.COPIES * o
        for i in (3, 1, 2, 0):
            self.local(i, o).wait()
            self.arrived(self.near.at[i, s], k + i)
            self.add(self.mine.at[i, s], self.near.at[i, s])
            if i == 3:
                self.begin(self.p0(3, s), self.side0.at[1, s], {"dp": self.dp ^ my}, k + 4)
                self.begin(self.p1(3, s), self.side1.at[1, s], {"dp": self.dp ^ mx}, k + 5)
            if i == 1:
                self.begin(self.p0(1, s), self.side0.at[0, s], {"dp": self.dp ^ my}, k + 6)
            if i == 2:
                self.begin(self.p1(2, s), self.side1.at[0, s], {"dp": self.dp ^ mx}, k + 7)

    def two(self, o):
        my, mx, _ = self.masks
        s, k = self.seat(o), self.COPIES * o
        self.arrived(self.side0.at[1, s], k + 4)
        self.add(self.p0(2, s), self.side0.at[1, s])
        self.begin(self.p0(2, s), self.side0.at[2, s], {"dp": self.dp ^ mx}, k + 8)
        self.arrived(self.side1.at[1, s], k + 5)
        self.add(self.p1(1, s), self.side1.at[1, s])
        self.begin(self.p1(1, s), self.side1.at[2, s], {"dp": self.dp ^ my}, k + 9)

    def three(self, o):
        s, k = self.seat(o), self.COPIES * o
        for ref, side, k1, k2 in ((self.p0(0, s), self.side0, k + 6, k + 8), (self.p1(0, s), self.side1, k + 7, k + 9)):
            self.arrived(side.at[0, s], k1)
            self.arrived(side.at[2, s], k2)
            ref[...] = (ref[...].astype(F32) + side[0, s].astype(F32) + side[2, s].astype(F32)).astype(BF)
        if o:
            self.begin(self.mine.at[0, s], self.far.at[o - 1], {"seq": s}, self.COPIES * self.nz + o)

    def four(self):
        out = self.mine[0, self.z].astype(F32)
        for o in range(1, self.nz):
            self.arrived(self.far.at[o - 1], self.COPIES * self.nz + o)
            out = out + self.far[o - 1].astype(F32)
        self.total[...] = out

    def done(self):
        for c in self.started:
            c.wait_send()


def reduce_kernel(nz, masks, n, *refs):
    srcs, totals, rest = refs[:n], refs[n : 2 * n], refs[2 * n :]
    dp, z = lax.axis_index("dp"), lax.axis_index("seq")
    greet(z, nz, dp, masks)
    jobs = []
    for i in range(n):
        part = rest[8 * i : 8 * i + 8]
        jobs.append(Reduce(srcs[i], totals[i], half_lanes(srcs[i].shape[-1]), nz, masks, part[:5], *part[5:]))
    order = list(range(1, nz)) + [0]
    for step in ("zero", "one", "two", "three"):
        for j in jobs:
            for o in order:
                getattr(j, step)(o)
    for j in jobs:
        j.four()
    for j in jobs:
        j.done()


def reduced(packs, nz, masks):
    scratch = []
    for p in packs:
        bufs, sems = Reduce.scratch(p.shape[-2:], half_lanes(p.shape[-1]), nz)
        scratch += bufs + sems
    return pl.pallas_call(
        functools.partial(reduce_kernel, nz, masks, len(packs)),
        out_shape=[jax.ShapeDtypeStruct(p.shape[-2:], F32) for p in packs],
        in_specs=[pl.BlockSpec(memory_space=pl.ANY)] * len(packs),
        out_specs=[pl.BlockSpec(memory_space=pltpu.VMEM)] * len(packs),
        scratch_shapes=scratch,
        compiler_params=pltpu.CompilerParams(collective_id=2, has_side_effects=True, vmem_limit_bytes=58 << 20),
        name="sum_packs",
    )(*packs)


def pack_qkv(w_qkv, gain):
    r = w_qkv.shape[0]
    body = jnp.concatenate([w_qkv[:, :1152], w_qkv[:, 1152:]], 0)
    return jnp.concatenate([body, jnp.pad(gain[:, None], ((0, r), (0, 127)))], 1)


def pack_out(w_out, gain):
    r = w_out.shape[0]
    body = jnp.concatenate([w_out[:, :384], w_out[:, 384:]], 0)
    return jnp.concatenate([body, jnp.pad(gain[:, None], ((0, r), (0, 127)))], 1)


def unpack_rows(total):
    r, c = total.shape[0] // 2, total.shape[1] - 128
    return jnp.concatenate([total[:r, :c], total[r:, :c]], 1), total[:r, c]


def pack_mlp(w_in, w_down):
    parts = (w_in[:, 0], w_in[:, 1], w_down.T)
    pads = jnp.zeros((w_in.shape[0], 128 - 3 * REST), BF)
    return jnp.concatenate([x[:, :MAIN] for x in parts] + [x[:, MAIN:] for x in parts] + [pads], 1)


def unpack_mlp(total):
    gate, up, down = [
        jnp.concatenate([total[:, MAIN * i : MAIN * i + MAIN], total[:, 3 * MAIN + REST * i : 3 * MAIN + REST * i + REST]], 1)
        for i in range(3)
    ]
    return jnp.stack([gate, up], 1), down.T


def whole_packs(w_qkv, w_out, attn_gain, mlp_gain, w_in, w_down):
    both = ("dp", "seq")

    def rows_of(w, gain, pack):
        w, gain = lax.all_gather(w, both, axis=0, tiled=True), lax.all_gather(gain, both, axis=0, tiled=True)
        shards = jax.vmap(pack)(w.reshape(GROUPS * LINE, SLIVER, -1), gain.reshape(GROUPS * LINE, SLIVER))
        return shards.reshape((GROUPS, LINE) + shards.shape[1:])

    mlp = pack_mlp(lax.all_gather(w_in, "dp", axis=0, tiled=True), lax.all_gather(w_down, "dp", axis=1, tiled=True))
    mlp = lax.all_gather(mlp, "seq", axis=0, tiled=False)
    mlp = mlp.reshape(LINE, GROUPS, BAND, -1).transpose(1, 0, 2, 3)
    return rows_of(w_qkv, attn_gain, pack_qkv), rows_of(w_out, mlp_gain, pack_out), mlp


def whole_sums(pq_g, po_g, pm_g):
    both = ("dp", "seq")
    found = []
    for pack in (pq_g, po_g):
        w, gain = jax.vmap(unpack_rows)(pack.reshape((GROUPS * LINE,) + pack.shape[2:]).astype(F32))
        found.append(lax.psum_scatter(w.reshape(WIDTH, -1), both, scatter_dimension=0, tiled=True))
        found.append(lax.psum_scatter(gain.reshape(WIDTH), both, scatter_dimension=0, tiled=True))
    mlp = pm_g.astype(F32).transpose(1, 0, 2, 3).reshape(LINE, WIDTH, -1)
    mlp = lax.psum_scatter(mlp, "seq", scatter_dimension=0, tiled=False)
    mlp = lax.psum_scatter(mlp, "dp", scatter_dimension=0, tiled=True)
    return found + list(unpack_mlp(mlp))


def on_device(tokens, w_qkv, w_out, attn_gain, mlp_gain, w_in, w_down, grad_out, *, dp, nz):
    rows = tokens.shape[0]
    masks = (dp // 2, dp // 4, 1) if dp == GROUPS and nz == LINE else None
    cos, sine = [jnp.asarray(t).reshape(nz, rows, 128) for t in rope_tables(nz * rows)]
    if masks:
        packs = [pack_qkv(w_qkv, attn_gain), pack_out(w_out, mlp_gain), pack_mlp(w_in, w_down)]
        mixed, lse, query, keys, values, firsts, wqkv, gain, po_all, pm_all = front(tokens, packs, cos, sine, nz, masks)
    else:
        pq_all, po_all, pm_all = whole_packs(w_qkv, w_out, attn_gain, mlp_gain, w_in, w_down)
        mixed, lse, query, keys, values, firsts, wqkv, gain = front(tokens, [pq_all], cos, sine, nz, None)
    out, gmid, gmixed, delta, po_g, pm_g = middle(tokens, mixed, grad_out, po_all, pm_all)
    gtok, pq_g = back(tokens, gmid, query, keys, values, firsts, wqkv, gain, gmixed, lse, delta, cos, sine, nz)
    if masks:
        sq, so, sm = reduced([pq_g, po_g, pm_g], nz, masks)
        g_qkv, g_gain_a = unpack_rows(sq)
        g_out, g_gain_m = unpack_rows(so)
        g_in, g_down = unpack_mlp(sm)
    else:
        g_qkv, g_gain_a, g_out, g_gain_m, g_in, g_down = whole_sums(pq_g, po_g, pm_g)
    return out, gtok, g_qkv, g_out, g_gain_a, g_gain_m, g_in, g_down


def solution(mesh):
    both = P(("dp", "seq"), None)
    vector = P(("dp", "seq"))
    w_in, w_down = P("dp", None, "seq"), P("seq", "dp")
    step = functools.partial(on_device, dp=mesh.shape["dp"], nz=mesh.shape["seq"])
    return jax.shard_map(
        step,
        mesh=mesh,
        in_specs=(both, both, both, vector, vector, w_in, w_down, both),
        out_specs=(both, both, both, both, vector, vector, w_in, w_down),
        check_vma=False,
    )
```

time: 1010 us -> 356 us (0.35)
  waiting for transfers between devices: 599 us -> 0 us
  Pallas kernels: 0 us -> 336 us
  matrix products: 166 us -> 0 us
  blocking collectives: 105 us -> 0 us
  other arithmetic: 57.6 us -> 2.69 us
  local copies, waits for them, and re-layouts: 46.9 us -> 15.2 us
  between operations: 14.9 us -> 0.79 us
    reduce_scatter x6 -> x0, waiting for transfers between devices: 355 us -> none  [the longest x1 125 us: on_device(): lax.psum_scatter(grad_w_qkv, ('dp', 'seq'), scatter_dimension=0, tiled=True)]
    pallas_call x0 -> x4, Pallas kernels: none -> 336 us  [the longest x1 141 us: front(): pl.pallas_call(functools.partial(front_kernel, nz, masks, rows), out_shap...]
    all_gather x6 -> x0, waiting for transfers between devices: 226 us -> none  [the longest x1 59.6 us: on_device(): rows_all = lax.all_gather(second_in, 'seq', axis=0, tiled=True)]
    dot_general x54 -> x0, matrix products: 166 us -> none  [the longest x6 23.6 us: attend(): jnp.einsum('hqk,khd->qhd', prob_vals, value_pair, preferred_element_type=...]
    unnamed x2 -> x0, blocking collectives: 81.7 us -> none
    all_gather x2 -> x0, blocking collectives: 23.7 us -> none  [the longest x1 12.7 us: on_device(): lax.all_gather(w_in, 'dp', axis=0, tiled=True)]
    convert_element_type x12 -> x0, other arithmetic: 20.8 us -> none  [the longest x6 12.3 us: attend_back(): grad_scores = (prob_vals * (grad_probs - jnp.sum(prob_vals * grad_probs,...]
    reduce_sum x12 -> x0, other arithmetic: 18.2 us -> none  [the longest x6 9.83 us: attend(): row_total = jnp.sum(expo_vals, -1, keepdims=True)]
  transfers between devices with their start and end apart: 14 -> 0, of which waited for: 14 -> 0; matrix products, arithmetic and copies ran while one was open for 13% -> 0% of each run, Pallas kernels for 0% -> 0%
where the time goes in v1:
time: 356 us; the launch traced here: 354 us
  Pallas kernels  336 us (94%)
  local copies, waits for them, and re-layouts  15.2 us (4%)
    pallas_call x1, Pallas kernels, front(): pl.pallas_call(functools.partial(front_kernel, nz, masks, rows), out_shap...  141 us
    pallas_call x1, Pallas kernels, back(): pl.pallas_call(functools.partial(back_kernel, nz, rows), out_shape=[shape...  86 us
    pallas_call x1, Pallas kernels, reduced(): pl.pallas_call(functools.partial(reduce_kernel, nz, masks, len(packs)), o...  80.6 us
    pallas_call x1, Pallas kernels, middle(): pl.pallas_call(functools.partial(middle_kernel, rows), out_shape=[shape((...  28.2 us

profile of v1, /device:TPU:0, one launch (start us, length us, event | category | flops | bytes accessed | tf_op | source)
XLA Modules:
  0.0 354.5 jit_solution(15986365192444644307)
XLA Ops:
  0.6 0.7 copy.25
  1.4 0.7 copy.26
  2.1 0.7 fusion.10
  2.9 0.6 fusion.3.refs_2_
  3.5 1.0 copy.29
  4.5 0.9 fusion.8
  5.4 0.7 fusion.1.refs_1_
  6.0 1.2 fusion.7
  7.4 0.8 concatenate.34.refs_3_
  8.2 140.9 %front.1 = (bf16[512,768]{1,0:T(8,128)(2,1)}, f32[16,512]{1,0:T(8,128)}, bf16[512,768]{1,0:T(8,128)(2,1)}, bf16[4,512,768]{2,1,0:T(8,128)(2,1)}, bf16[4,512,768]...) custom-call(bf16[512,768]{1,0:T(8,128)(2,1)} %tok.3, ...), custom_call_target="tpu_custom_call" | custom-call | flops 14000000000 | bytes 40000000 | tf_op jit(solution)/shard_map/front/pallas_call | solution.py:416
  149.0 28.2 %middle.1 = (bf16[512,768]{1,0:T(8,128)(2,1)}, f32[512,768]{1,0:T(8,128)}, bf16[512,768]{1,0:T(8,128)(2,1)}, f32[16,512]{1,0:T(8,128)}, bf16[8,4,48,512]{3,2,1,0...) custom-call(bf16[512,768]{1,0:T(8,128)(2,1)} %tok.3, bf16[512,768]{1,0:T(8,128)(2,1)} %get-tuple-element.29.mixed, ...), custom_call_target="tpu_custom_call" | custom-call | flops 11000000512 | bytes 25000000 | tf_op jit(solution)/shard_map/middle/pallas_call | solution.py:549
  177.2 86.0 %back.1 = (bf16[512,768]{1,0:T(8,128)(2,1)}, bf16[8,4,48,1280]{3,2,1,0:T(8,128)(2,1)}) custom-call(bf16[512,768]{1,0:T(8,128)(2,1)} %tok.3, f32[512,768]{1,0:T(8,128)} %get-tuple-element.33.gmid, bf16[512,768]{1,0:T(8,128)(2,1)} %get-tuple-element.34.query, bf16[4,512,768]{2,1,0:T(8,128)(2,1)} %get-tuple-element.35.keys, ...), custom_call_target="tpu_custom_call" | custom-call | flops 24000000000 | bytes 40000000 | tf_op jit(solution)/shard_map/back/pallas_call | solution.py:691
  263.3 80.6 %sum_packs.1 = (f32[48,1280]{1,0:T(8,128)}, f32[48,512]{1,0:T(8,128)}, f32[96,896]{1,0:T(8,128)}) custom-call(bf16[8,4,48,1280]{3,2,1,0:T(8,128)(2,1)} %get-tuple-element.44.refs_0_, bf16[8,4,48,512]{3,2,1,0:T(8,128)(2,1)} %get-tuple-element.45.refs_1_, bf16[8,4,96,896]{3,2,1,0:T(8,128)(2,1)} %get-tuple-element.46.refs_2_), custom_call_target="tpu_custom_call" | custom-call | tf_op jit(solution)/shard_map/sum_packs/pallas_call | solution.py:840
  343.9 0.0 copy-start
  343.9 1.4 slice_reduce_fusion.1
  345.3 1.0 fusion.6
  346.3 0.7 pad_maximum_fusion.1
  347.0 1.3 slice_reduce_fusion
  348.3 0.8 fusion.9
  349.1 0.6 pad_maximum_fusion.2
  349.8 1.0 fusion.5
  350.8 1.0 fusion.4
  351.8 0.8 copy.31
  352.6 0.9 copy.30
  353.6 0.0 copy-done
  353.6 0.9 copy.37
  (12 shorter events, 0.1 us)
Async XLA Ops:
  343.9 9.7 %copy-start = (bf16[512,768]{1,0:T(8,128)(2,1)S(1)}, bf16[512,768]{1,0:T(8,128)(2,1)}, u32[]{:S(2)}) copy-start(bf16[512,768]{1,0:T(8,128)(2,1)} %get-tuple-element.93) | copy-start | bytes 2359300

commit v2 on v1

--- a/solution.py
+++ b/solution.py
@@ -82,24 +82,34 @@
     return inv * (d - jnp.mean(d, -1, keepdims=True) - hat * jnp.mean(d * hat, -1, keepdims=True))
 
 
-def chunk_at(z, t, nz):
-    both = jnp.minimum(z, nz - 1 - z)
-    near = jnp.where(lax.rem(t, 2) == 1, z - (t + 1) // 2, z + (t + 1) // 2)
-    far = jnp.where(z < nz - 1 - z, z + t - both, z - t + both)
-    return jnp.where(t <= 2 * both, near, far)
-
-
 def remote(src, dst, send, recv, device):
     return pltpu.make_async_remote_copy(src, dst, send, recv, device_id=device, device_id_type=MESH)
 
 
-def greet(z, nz, dp, masks):
-    bar = pltpu.get_barrier_semaphore()
-    for o in range(1, nz):
-        pl.semaphore_signal(bar, inc=1, device_id={"seq": lax.rem(z + o, nz)}, device_id_type=MESH)
-    for m in masks:
-        pl.semaphore_signal(bar, inc=1, device_id={"dp": dp ^ m}, device_id_type=MESH)
-    pl.semaphore_wait(bar, nz - 1 + len(masks))
+class Place:
+    def __init__(self, nz):
+        self.dp, self.z = lax.axis_index("dp"), lax.axis_index("seq")
+        self.nz = nz
+        upper = self.z // (nz // 2)
+        self.moves = lax.rem(self.dp, 2) != upper
+        self.stays = lax.rem(self.dp, 2) == upper
+        self.shard = jnp.where(self.moves, nz - 1 - self.z, self.z)
+        self.opposite = {"dp": self.dp ^ 1, "seq": nz - 1 - self.z}
+        self.twin = {"dp": self.dp ^ 1}
+        self.beside = {"seq": self.z ^ 1}
+
+    def greet(self, masks):
+        bar = pltpu.get_barrier_semaphore()
+
+        def hello(device):
+            pl.semaphore_signal(bar, inc=1, device_id=device, device_id_type=MESH)
+
+        for o in range(1, self.nz):
+            hello({"seq": lax.rem(self.z + o, self.nz)})
+        for m in masks:
+            hello({"dp": self.dp ^ m})
+        hello(self.opposite)
+        pl.semaphore_wait(bar, self.nz + len(masks))
 
 
 class Gather:
@@ -121,10 +131,9 @@
     def copy(self, src, dst, device, k):
         return remote(src, dst, self.send.at[k], self.recv.at[k], device)
 
-    def begin(self, src, dst, device, k):
-        c = self.copy(src, dst, device, k)
-        c.start()
-        self.started.append(c)
+    def begin(self, src, dst, device, k, p=None):
+        self.copy(src, dst, device, k).start()
+        self.started.append((k, p))
 
     def arrived(self, ref, k):
         self.copy(ref, ref, {"dp": self.dp ^ self.masks[0]}, k).wait_recv()
@@ -145,7 +154,7 @@
 
     def forward(self, src, d, s, mask, k, p=None):
         dst = self.out.at[d, s]
-        self.begin(self.part(src, p), self.part(dst, p), {"dp": self.dp ^ mask}, k)
+        self.begin(self.part(src, p), self.part(dst, p), {"dp": self.dp ^ mask}, k, p)
 
     def first(self, o):
         my, mx, mc = self.masks
@@ -185,8 +194,9 @@
             self.arrived(self.part(self.out.at[self.dp ^ mc ^ my ^ mx, s], p), self.key(o, k))
 
     def done(self):
-        for c in self.started:
-            c.wait_send()
+        for k, p in self.started:
+            ref = self.part(self.out.at[self.dp, self.z], p)
+            self.copy(ref, ref, {"dp": self.dp ^ self.masks[0]}, k).wait_send()
 
 
 def half_lanes(width):
@@ -196,22 +206,31 @@
 def front_kernel(nz, masks, rows, *refs):
     fused = masks is not None
     if fused:
-        (tok, pq, po, pm, cos, sine, mixed, lse, query, keys, values, firsts, wqkv, gain, po_all, pm_all, tok_all, pq_all,
-         gcol, acc, top, total, tsend, trecv, qs, qr, os_, or_, ms, mr, loc) = refs
+        (tok, gout, pq, po, pm, cos, sine, mixed, lse, query, gain, tok_own, gout_own, keys, values, firsts, wqkv, po_all, pm_all,
+         tok_all, kb, vb, fb, wq, gcol, acc, top, total, tsend, trecv, loc, pq_all, qs, qr, os_, or_, ms, mr) = refs
     else:
-        (tok, pq_all, cos, sine, mixed, lse, query, keys, values, firsts, wqkv, gain, tok_all,
-         gcol, acc, top, total, tsend, trecv, loc) = refs
-    dp, z = lax.axis_index("dp"), lax.axis_index("seq")
-
-    own = pltpu.make_async_copy(tok, tok_all.at[z], loc.at[0])
-    own.start()
+        (tok, gout, pq_all, cos, sine, mixed, lse, query, gain, tok_own, gout_own, keys, values, firsts, wqkv,
+         tok_all, kb, vb, fb, wq, gcol, acc, top, total, tsend, trecv, loc) = refs
+    me = Place(nz)
+    own = me.shard
+
+    def here(src, dst, k):
+        return pltpu.make_async_copy(src, dst, loc.at[k])
+
+    def there(src, dst, device, k):
+        return remote(src, dst, tsend.at[k], trecv.at[k], device)
+
+    @pl.when(me.stays)
+    def _():
+        here(tok, tok_all.at[own], 0).start()
+        here(gout, gout_own, 1).start()
+
     if fused:
-        locals_ = []
-        for i, (src, out) in enumerate(((pq, pq_all), (po, po_all), (pm, pm_all))):
-            c = pltpu.make_async_copy(src, out.at[dp, z], loc.at[1 + i])
+        locals_ = [here(src, out.at[me.dp, me.z], 2 + i) for i, (src, out) in enumerate(((pq, pq_all), (po, po_all), (pm, pm_all)))]
+        for c in locals_:
             c.start()
-            locals_.append(c)
-        greet(z, nz, dp, masks)
+    me.greet(masks or (1,))
+    if fused:
         packs = [
             Gather(pq, pq_all, half_lanes(pq.shape[-1]), nz, masks, qs, qr),
             Gather(po, po_all, half_lanes(po.shape[-1]), nz, masks, os_, or_),
@@ -220,31 +239,17 @@
         first, *later = packs
         first.along()
         first.first(0)
-    else:
-        bar = pltpu.get_barrier_semaphore()
-        for o in range(1, nz):
-            pl.semaphore_signal(bar, inc=1, device_id={"seq": lax.rem(z + o, nz)}, device_id_type=MESH)
-        pl.semaphore_wait(bar, nz - 1)
-
-    def hop(src, c, left):
-        to = z - 1 if left else z + 1
-        k = nz if left else c
-        if src is None:
-            src = tok_all.at[c]
-            k = c
-        return remote(src, tok_all.at[c], tsend.at[k], trecv.at[c], {"seq": to})
-
-    @pl.when(z + 1 < nz)
-    def _():
-        hop(tok, z, False).start()
-
-    @pl.when(z > 0)
-    def _():
-        hop(tok, z, True).start()
+
+    @pl.when(me.stays)
+    def _():
+        there(tok, tok_all.at[own], me.twin, 1).start()
+        there(tok, tok_all.at[own], me.beside, 2).start()
+
+    @pl.when(me.moves)
+    def _():
+        there(tok, tok_all.at[me.z], me.opposite, 0).start()
 
     if fused:
-        for g in later:
-            g.along()
         first.second(0)
         for o in range(1, nz):
             first.first(o)
@@ -252,64 +257,74 @@
             first.second(o)
         for o in range(nz):
             first.third(o)
+
+    @pl.when(me.moves)
+    def _():
+        there(tok, tok_all.at[own], me.opposite, 0).wait_recv()
+        there(tok_all.at[own], tok_all.at[own], me.twin, 1).start()
+        there(tok_all.at[own], tok_all.at[own], me.beside, 2).start()
+        there(gout, gout_own, me.opposite, 4).start()
+
+    @pl.when(me.stays)
+    def _():
+        here(tok, tok_all.at[own], 0).wait()
+
+    here(tok_all.at[own], tok_own, 5).start()
+    if fused:
         for g in later:
-            for o in range(nz):
-                g.first(o)
+            g.along()
+            g.first(0)
+        locals_[0].wait()
         for o in range(nz):
             first.finish(o)
-        for c in locals_:
-            c.wait()
-    own.wait()
 
     half = 1152
 
     def build(g, _):
         slabs = [pq_all[g, s].astype(F32) for s in range(LINE)]
         band = pl.ds(pl.multiple_of(g * BAND, BAND), BAND)
-        wqkv[band, :half] = jnp.concatenate([x[:SLIVER, :half] for x in slabs], 0).astype(BF)
-        wqkv[band, half:] = jnp.concatenate([x[SLIVER:, :half] for x in slabs], 0).astype(BF)
+        wq[band, :half] = jnp.concatenate([x[:SLIVER, :half] for x in slabs], 0).astype(BF)
+        wq[band, half:] = jnp.concatenate([x[SLIVER:, :half] for x in slabs], 0).astype(BF)
         gcol[band, :] = jnp.concatenate([x[:SLIVER, half:] for x in slabs], 0)
         return 0
 
     lax.fori_loop(0, GROUPS, build, 0)
+    here(wq, wqkv, 6).start()
     gain[...] = gcol[...].T[:8]
 
     def norm_chunk(c):
         def block(i, _):
             at = pl.ds(pl.multiple_of(i * 64, 64), 64)
             hat, _ = normed(tok_all[c, at, :].astype(F32))
-            firsts[c, at, :] = (hat * gain[0:1, :]).astype(BF)
+            fb[c, at, :] = (hat * gain[0:1, :]).astype(BF)
             return 0
 
         lax.fori_loop(0, rows // 64, block, 0)
+        here(fb.at[c], firsts.at[c], 7 + c).start()
 
     def project(c, j, base):
-        return dot(firsts[c], wqkv[:, base + 256 * j : base + 256 * j + 256], NN)
-
-    norm_chunk(z)
+        return dot(fb[c], wq[:, base + 256 * j : base + 256 * j + 256], NN)
+
+    norm_chunk(own)
     for j in range(3):
-        u = project(z, j, 0)
+        u = project(own, j, 0)
         for i in range(2):
-            tile = rope(u[:, 128 * i : 128 * i + 128], cos[z], sine[z])
+            tile = rope(u[:, 128 * i : 128 * i + 128], cos[own], sine[own])
             query[:, 256 * j + 128 * i : 256 * j + 128 * i + 128] = (tile * (SCALE * LOG2E)).astype(BF)
     acc[...] = jnp.zeros_like(acc)
     total[...] = jnp.zeros_like(total)
     top[...] = jnp.full_like(top, -1e30)
 
     def visit(t, _):
-        c = chunk_at(z, t, nz)
+        c = jnp.where(t == 0, own, jnp.where(t == 1, own ^ 3, jnp.where(t == 2, own ^ 1, own ^ 2)))
 
         @pl.when(t > 0)
         def _():
-            remote(tok_all.at[c], tok_all.at[c], tsend.at[c], trecv.at[c], {"seq": lax.rem(z + 1, nz)}).wait_recv()
-
-            @pl.when((c < z) & (z + 1 < nz))
+            there(tok_all.at[c], tok_all.at[c], me.twin, t).wait_recv()
+
+            @pl.when(t == 2)
             def _():
-                hop(None, c, False).start()
-
-            @pl.when((c > z) & (z > 0))
-            def _():
-                hop(None, c, True).start()
+                there(tok_all.at[c], tok_all.at[c], me.twin, 3).start()
 
             norm_chunk(c)
 
@@ -317,11 +332,13 @@
             u = project(c, j, WIDTH)
             for i in range(2):
                 at = 256 * j + 128 * i
-                keys[c, :, at : at + 128] = rope(u[:, 128 * i : 128 * i + 128], cos[c], sine[c]).astype(BF)
-            values[c, :, 256 * j : 256 * j + 256] = project(c, j, 2 * WIDTH).astype(BF)
+                kb[c, :, at : at + 128] = rope(u[:, 128 * i : 128 * i + 128], cos[c], sine[c]).astype(BF)
+            vb[c, :, 256 * j : 256 * j + 256] = project(c, j, 2 * WIDTH).astype(BF)
+        here(kb.at[c], keys.at[c], 7 + nz + c).start()
+        here(vb.at[c], values.at[c], 7 + 2 * nz + c).start()
 
         def pair(hp, _):
-            q, k, v = query[:, lanes_of(hp)], keys[c, :, lanes_of(hp)], values[c, :, lanes_of(hp)]
+            q, k, v = query[:, lanes_of(hp)], kb[c, :, lanes_of(hp)], vb[c, :, lanes_of(hp)]
             for h in range(2):
                 mask = (lane_iota() < 64) if h == 0 else (lane_iota() >= 64)
                 s = dot(k, jnp.where(mask, q, jnp.zeros_like(q)), NT)
@@ -337,6 +354,26 @@
             return 0
 
         lax.fori_loop(0, PAIRS, pair, 0)
+        if fused:
+
+            @pl.when(t == 1)
+            def _():
+                for g in later:
+                    for o in range(1, nz):
+                        g.first(o)
+
+            @pl.when(t == 2)
+            def _():
+                for g in later:
+                    for o in range(nz):
+                        g.second(o)
+
+            @pl.when(t == 3)
+            def _():
+                for g in later:
+                    for o in range(nz):
+                        g.third(o)
+
         return 0
 
     lax.fori_loop(0, nz, visit, 0)
@@ -351,68 +388,57 @@
     if fused:
         for g in later:
             for o in range(nz):
-                g.second(o)
-        for g in later:
-            for o in range(nz):
-                g.third(o)
-        for g in later:
-            for o in range(nz):
                 g.finish(o)
         for g in packs:
             g.done()
-
-    @pl.when(z + 1 < nz)
-    def _():
-        hop(tok, z, False).wait_send()
-
-    @pl.when(z > 0)
-    def _():
-        hop(tok, z, True).wait_send()
-
-    for t in range(1, nz):
-        c = chunk_at(z, t, nz)
-
-        @pl.when(((c < z) & (z + 1 < nz)) | ((c > z) & (z > 0)))
-        def _(c=c):
-            hop(None, c, False).wait_send()
-
-
-def front(tok, packs, cos, sine, nz, masks):
+        for c in locals_[1:]:
+            c.wait()
+    there(tok, tok_all.at[own], me.twin, 1).wait_send()
+    there(tok, tok_all.at[own], me.beside, 2).wait_send()
+    there(tok_all.at[own], tok_all.at[own], me.twin, 3).wait_send()
+
+    @pl.when(me.moves)
+    def _():
+        there(tok, tok_all.at[me.z], me.opposite, 0).wait_send()
+        there(gout, gout_own, me.opposite, 4).wait()
+
+    @pl.when(me.stays)
+    def _():
+        here(gout, gout_own, 1).wait()
+
+    here(tok_all.at[own], tok_own, 5).wait()
+    here(wq, wqkv, 6).wait()
+    for c in range(nz):
+        for i, (buf, dst) in enumerate(((fb, firsts), (kb, keys), (vb, values))):
+            here(buf.at[c], dst.at[c], 7 + nz * i + c).wait()
+
+
+def front(tok, gout, packs, cos, sine, nz, masks):
     rows = tok.shape[0]
     fused = masks is not None
     vmem, anyspace = pl.BlockSpec(memory_space=pltpu.VMEM), pl.BlockSpec(memory_space=pl.ANY)
-    shape = jax.ShapeDtypeStruct
-    outs = [
-        shape((rows, WIDTH), BF),
-        shape((16, rows), F32),
-        shape((rows, WIDTH), BF),
-        shape((nz, rows, WIDTH), BF),
-        shape((nz, rows, WIDTH), BF),
-        shape((nz, rows, WIDTH), BF),
-        shape((WIDTH, 3 * WIDTH), BF),
-        shape((8, WIDTH), F32),
+    shape, vm = jax.ShapeDtypeStruct, pltpu.VMEM
+    outs = [shape((rows, WIDTH), BF), shape((16, rows), F32), shape((rows, WIDTH), BF), shape((8, WIDTH), F32)]
+    outs += [shape((rows, WIDTH), BF)] * 2 + [shape((nz, rows, WIDTH), BF)] * 3 + [shape((WIDTH, 3 * WIDTH), BF)]
+    out_specs = [vmem] * 4 + [anyspace] * 6
+    scratch = [vm((nz, rows, WIDTH), BF)] * 4 + [
+        vm((WIDTH, 3 * WIDTH), BF),
+        vm((WIDTH, 128), F32),
+        vm((WIDTH, rows), F32),
+        vm((16, rows), F32),
+        vm((16, rows), F32),
+        pltpu.SemaphoreType.DMA((5,)),
+        pltpu.SemaphoreType.DMA((5,)),
+        pltpu.SemaphoreType.DMA((7 + 3 * nz,)),
     ]
-    out_specs = [vmem] * 8
-    scratch = [pltpu.VMEM((nz, rows, WIDTH), BF)]
     if fused:
         pq, po, pm = packs
         outs += [shape((GROUPS, nz) + po.shape, BF), shape((GROUPS, nz) + pm.shape, BF)]
         out_specs += [anyspace] * 2
-        in_specs = [anyspace] * 4 + [vmem] * 2
-        scratch += [pltpu.VMEM((GROUPS, nz) + pq.shape, BF)]
+        in_specs = [anyspace] * 5 + [vmem] * 2
+        scratch += [vm((GROUPS, nz) + pq.shape, BF)] + [pltpu.SemaphoreType.DMA((Gather.sems(nz),)) for _ in range(6)]
     else:
-        in_specs = [anyspace] + [vmem] * 3
-    scratch += [
-        pltpu.VMEM((WIDTH, 128), F32),
-        pltpu.VMEM((WIDTH, rows), F32),
-        pltpu.VMEM((16, rows), F32),
-        pltpu.VMEM((16, rows), F32),
-        pltpu.SemaphoreType.DMA((nz + 1,)),
-        pltpu.SemaphoreType.DMA((nz,)),
-    ]
-    if fused:
-        scratch += [pltpu.SemaphoreType.DMA((Gather.sems(nz),)) for _ in range(6)]
-    scratch += [pltpu.SemaphoreType.DMA((4,))]
+        in_specs = [anyspace] * 2 + [vmem] * 3
     return pl.pallas_call(
         functools.partial(front_kernel, nz, masks, rows),
         out_shape=outs,
@@ -422,7 +448,7 @@
         compiler_params=pltpu.CompilerParams(collective_id=0, has_side_effects=True, vmem_limit_bytes=58 << 20),
         cost_estimate=pl.CostEstimate(flops=14_000_000_000, bytes_accessed=40_000_000, transcendentals=13_000_000),
         name="front",
-    )(tok, *packs, cos, sine)
+    )(tok, gout, *packs, cos, sine)
 
 
 def middle_kernel(rows, tok, mixed, gout, po_all, pm_all, out, gmid, gmixed, delta, po_g, pm_g,
@@ -582,26 +608,186 @@
     )(tok, mixed, gout, po_all, pm_all)
 
 
-def back_kernel(nz, rows, tok, gmid, query, keys, values, firsts, wqkv, gain, gmixed, lse, delta, cos, sine,
-                gtok, pq_g, dq, dkv, dx, dw, posted, landed, gcol, send, recv):
-    z = lax.axis_index("seq")
-    bar = pltpu.get_barrier_semaphore()
-    for o in range(1, nz):
-        pl.semaphore_signal(bar, inc=1, device_id={"seq": lax.rem(z + o, nz)}, device_id_type=MESH)
-    pl.semaphore_wait(bar, nz - 1)
+class Reduce:
+    COPIES = 10
+
+    def __init__(self, src, total, cut, nz, masks, bufs, send, recv, loc=None):
+        self.src, self.total, self.cut, self.nz, self.masks = src, total, cut, nz, masks
+        self.near, self.side0, self.side1, self.far, *mine = bufs
+        self.mine = mine[0] if mine else None
+        self.send, self.recv, self.loc = send, recv, loc
+        self.dp, self.z = lax.axis_index("dp"), lax.axis_index("seq")
+        my, mx, mc = masks
+        self.turns = (0, my, mx, my ^ mx)
+        self.started = []
+
+    @staticmethod
+    def scratch(shape, nz, held):
+        r, c = shape
+        cut = half_lanes(c)
+        bufs = [
+            pltpu.VMEM((4, nz, r, c), BF),
+            pltpu.VMEM((3, nz, r, cut), BF),
+            pltpu.VMEM((3, nz, r, c - cut), BF),
+            pltpu.VMEM((nz - 1, r, c), BF),
+        ]
+        sems = [pltpu.SemaphoreType.DMA((Reduce.COPIES * nz + nz,))] * 2
+        if not held:
+            bufs += [pltpu.VMEM((4, nz, r, c), BF)]
+            sems += [pltpu.SemaphoreType.DMA((4 * nz,))]
+        return bufs, sems
+
+    def begin(self, src, dst, device, k):
+        remote(src, dst, self.send.at[k], self.recv.at[k], device).start()
+        self.started.append((k, src.shape[-1]))
+
+    def arrived(self, ref, k):
+        remote(ref, ref, self.send.at[k], self.recv.at[k], {"dp": self.dp ^ self.masks[2]}).wait_recv()
+
+    def seat(self, o):
+        return lax.rem(self.z + o, self.nz)
+
+    def held(self, i, s):
+        return self.mine.at[i, s] if self.mine is not None else self.src.at[self.dp ^ self.turns[i], s]
+
+    def local(self, i, o):
+        s = self.seat(o)
+        return pltpu.make_async_copy(self.src.at[self.dp ^ self.turns[i], s], self.mine.at[i, s], self.loc.at[4 * o + i])
+
+    def zero(self, o):
+        s, mc = self.seat(o), self.masks[2]
+        for i in (3, 1, 2, 0):
+            if self.mine is not None:
+                self.local(i, o).start()
+            self.begin(self.src.at[self.dp ^ mc ^ self.turns[i], s], self.near.at[i, s], {"dp": self.dp ^ mc}, self.COPIES * o + i)
+
+    def add(self, ref, other):
+        ref[...] = (ref[...].astype(F32) + other[...].astype(F32)).astype(BF)
+
+    def p0(self, i, s):
+        return self.held(i, s).at[:, pl.ds(0, self.cut)]
+
+    def p1(self, i, s):
+        return self.held(i, s).at[:, pl.ds(self.cut, self.src.shape[-1] - self.cut)]
+
+    def one(self, o):
+        my, mx, _ = self.masks
+        s, k = self.seat(o), self.COPIES * o
+        for i in (3, 1, 2, 0):
+            if self.mine is not None:
+                self.local(i, o).wait()
+            self.arrived(self.near.at[i, s], k + i)
+            self.add(self.held(i, s), self.near.at[i, s])
+            if i == 3:
+                self.begin(self.p0(3, s), self.side0.at[1, s], {"dp": self.dp ^ my}, k + 4)
+                self.begin(self.p1(3, s), self.side1.at[1, s], {"dp": self.dp ^ mx}, k + 5)
+            if i == 1:
+                self.begin(self.p0(1, s), self.side0.at[0, s], {"dp": self.dp ^ my}, k + 6)
+            if i == 2:
+                self.begin(self.p1(2, s), self.side1.at[0, s], {"dp": self.dp ^ mx}, k + 7)
+
+    def two(self, o):
+        my, mx, _ = self.masks
+        s, k = self.seat(o), self.COPIES * o
+        self.arrived(self.side0.at[1, s], k + 4)
+        self.add(self.p0(2, s), self.side0.at[1, s])
+        self.begin(self.p0(2, s), self.side0.at[2, s], {"dp": self.dp ^ mx}, k + 8)
+        self.arrived(self.side1.at[1, s], k + 5)
+        self.add(self.p1(1, s), self.side1.at[1, s])
+        self.begin(self.p1(1, s), self.side1.at[2, s], {"dp": self.dp ^ my}, k + 9)
+
+    def three(self, o):
+        s, k = self.seat(o), self.COPIES * o
+        for ref, side, k1, k2 in ((self.p0(0, s), self.side0, k + 6, k + 8), (self.p1(0, s), self.side1, k + 7, k + 9)):
+            self.arrived(side.at[0, s], k1)
+            self.arrived(side.at[2, s], k2)
+            ref[...] = (ref[...].astype(F32) + side[0, s].astype(F32) + side[2, s].astype(F32)).astype(BF)
+        if o:
+            self.begin(self.held(0, s), self.far.at[o - 1], {"seq": s}, self.COPIES * self.nz + o)
+
+    def four(self):
+        out = self.held(0, self.z)[...].astype(F32)
+        for o in range(1, self.nz):
+            self.arrived(self.far.at[o - 1], self.COPIES * self.nz + o)
+            out = out + self.far[o - 1].astype(F32)
+        self.total[...] = out
+
+    def done(self):
+        for k, width in self.started:
+            whole = width == self.src.shape[-1]
+            ref = self.near.at[0, 0] if whole else (self.side0 if k % self.COPIES in (4, 6, 8) else self.side1).at[0, 0]
+            remote(ref, ref, self.send.at[k], self.recv.at[k], {"dp": self.dp ^ self.masks[2]}).wait_send()
+
+
+def back_kernel(nz, masks, rows, *refs):
+    fused = masks is not None
+    (tok, gmid, out_own, query, keys, values, firsts, wqkv, gain, gmixed, lse, delta, cos, sine), refs = refs[:14], refs[14:]
+    if fused:
+        (po_g, pm_g, gtok, out, sq, so, sm), refs = refs[:7], refs[7:]
+    else:
+        (gtok, out, pq_g), refs = refs[:3], refs[3:]
+    (kb, vb, fb, ft, wq, dq, dkv, dx, dw, sent, landed, gown, gcol, send, recv, loc), refs = refs[:16], refs[16:]
+    me = Place(nz)
+    own = me.shard
+    me.greet(masks or (1,))
+
+    def here(src, dst, k):
+        return pltpu.make_async_copy(src, dst, loc.at[k])
+
+    def there(src, dst, device, k):
+        return remote(src, dst, send.at[k], recv.at[k], device)
+
+    def chunk(t):
+        return jnp.where(t == 0, own ^ 2, jnp.where(t == 1, own ^ 1, jnp.where(t == 2, own ^ 3, own)))
+
+    def fetch(t):
+        c, slot = chunk(t), lax.rem(t, 2)
+        return [here(src.at[c], buf.at[slot], 3 * slot + i) for i, (src, buf) in enumerate(((keys, kb), (values, vb), (firsts, fb)))]
+
+    for c in fetch(0):
+        c.start()
+    here(wqkv, wq, 6).start()
+    jobs = []
+    if fused:
+        pq_g, refs = refs[0], refs[1:]
+        last = Reduce(pq_g, sq, half_lanes(pq_g.shape[-1]), nz, masks, refs[:4], *refs[4:6])
+        refs = refs[6:]
+        for src, total in ((po_g, so), (pm_g, sm)):
+            jobs.append(Reduce(src, total, half_lanes(src.shape[-1]), nz, masks, refs[:5], *refs[5:8]))
+            refs = refs[8:]
+    order = list(range(1, nz)) + [0]
+
+    def advance(which, step):
+        for j in which:
+            for o in order:
+                getattr(j, step)(o)
+
+    advance(jobs, "zero")
+
+    @pl.when(me.moves)
+    def _():
+        there(out_own, out, me.opposite, 3).start()
+
+    @pl.when(me.stays)
+    def _():
+        here(out_own, out, 7).start()
+
     dq[...] = jnp.zeros_like(dq)
     dw[...] = jnp.zeros_like(dw)
 
-    def post(c):
-        k = lax.rem(z - c + nz, nz) - 1
-        return remote(posted.at[k], landed.at[k], send.at[k], recv.at[k], {"seq": c})
-
     def visit(t, _):
-        c = chunk_at(z, nz - 1 - t, nz)
+        c, slot = chunk(t), lax.rem(t, 2)
+        for f in fetch(t):
+            f.wait()
+
+        @pl.when(t + 1 < nz)
+        def _():
+            for f in fetch(t + 1):
+                f.start()
 
         def pair(hp, _):
             at = lanes_of(hp)
-            q, g, k, v = query[:, at], gmixed[:, at], keys[c, :, at], values[c, :, at]
+            q, g, k, v = query[:, at], gmixed[:, at], kb[slot, :, at], vb[slot, :, at]
             dk = dv = None
             for h in range(2):
                 mask = (lane_iota() < 64) if h == 0 else (lane_iota() >= 64)
@@ -621,25 +807,43 @@
 
         lax.fori_loop(0, PAIRS, pair, 0)
 
+        @pl.when(t == 0)
+        def _():
+            here(wqkv, wq, 6).wait()
+
         for j in range(3):
             at = slice(256 * j, 256 * j + 256)
-            x = dot(dkv[...], wqkv[at, WIDTH:], NT)
-            dx[:, at] = x
-
-        @pl.when(c != z)
+            dx[:, at] = dot(dkv[...], wq[at, WIDTH:], NT)
+
+        @pl.when(lax.rem(t, 2) == 0)
         def _():
-            k = lax.rem(z - c + nz, nz) - 1
-            posted[k] = dx[...].astype(BF)
-            post(c).start()
+            sent[t] = dx[...].astype(BF)
+            there(sent.at[t], landed.at[t], me.twin, t).start()
+
+        @pl.when(t == 1)
+        def _():
+            there(sent.at[0], landed.at[0], me.twin, 0).wait_recv()
+            sent[1] = (dx[...] + landed[0].astype(F32)).astype(BF)
+            there(sent.at[1], landed.at[1], me.beside, 1).start()
+
+        for j in range(6):
+            ft[128 * j : 128 * j + 128, :] = fb[slot, :, 128 * j : 128 * j + 128].T
 
         def weigh(i, _):
             at, to = lanes_of(i, 256), lanes_of(i + 3, 256)
             for j in range(2):
                 r = slice(384 * j, 384 * j + 384)
-                dw[r, to] += dot(firsts[c, :, r], dkv[:, at], TN)
+                dw[r, to] += dot(ft[r, :], dkv[:, at], NN)
             return 0
 
         lax.fori_loop(0, 6, weigh, 0)
+        if fused:
+            for k, step in enumerate(("one", "two", "three")):
+
+                @pl.when(t == k)
+                def _(step=step):
+                    advance(jobs, step)
+
         return 0
 
     lax.fori_loop(0, nz, visit, 0)
@@ -647,27 +851,34 @@
     for hp in range(PAIRS):
         at = slice(128 * hp, 128 * hp + 128)
         u = dq[at, :].T * SCALE
-        dkv[:, at] = rope_back(u, cos[z], sine[z]).astype(BF)
+        dkv[:, at] = rope_back(u, cos[own], sine[own]).astype(BF)
     for j in range(3):
         at = slice(256 * j, 256 * j + 256)
-        dx[:, at] += dot(dkv[:, :WIDTH], wqkv[at, :WIDTH], NT)
+        dx[:, at] += dot(dkv[:, :WIDTH], wq[at, :WIDTH], NT)
         for i in range(2):
             r = slice(384 * i, 384 * i + 384)
-            dw[r, at] = dot(firsts[z, :, r], dkv[:, at], TN)
-
-    for o in range(1, nz):
-        post(lax.rem(z + nz - o, nz)).wait_recv()
+            dw[r, at] = dot(ft[r, :], dkv[:, at], NN)
+
+    there(sent.at[1], landed.at[1], me.beside, 1).wait_recv()
+    there(sent.at[2], landed.at[2], me.twin, 2).wait_recv()
 
     def norm_block(i, dgain):
         at = pl.ds(pl.multiple_of(i * 64, 64), 64)
-        dy = dx[at, :]
-        for k in range(nz - 1):
-            dy = dy + landed[k, at, :].astype(F32)
+        dy = dx[at, :] + landed[1, at, :].astype(F32) + landed[2, at, :].astype(F32)
         h, r = normed(tok[at, :].astype(F32))
-        gtok[at, :] = (gmid[at, :] + norm_back(dy, gain[0:1, :], h, r)).astype(BF)
+        gown[at, :] = (gmid[at, :] + norm_back(dy, gain[0:1, :], h, r)).astype(BF)
         return dgain + jnp.sum(dy * h, 0, keepdims=True)
 
     dgain = lax.fori_loop(0, rows // 64, norm_block, jnp.zeros((1, WIDTH), F32))
+
+    @pl.when(me.moves)
+    def _():
+        there(gown, gtok, me.opposite, 4).start()
+
+    @pl.when(me.stays)
+    def _():
+        here(gown, gtok, 8).start()
+
     row = lax.broadcasted_iota(jnp.int32, (128, WIDTH), 0)
     gcol[...] = jnp.where(row == 0, dgain, 0.0).T
 
@@ -680,172 +891,73 @@
         return 0
 
     lax.fori_loop(0, GROUPS, pack, 0)
-    for o in range(1, nz):
-        post(lax.rem(z + nz - o, nz)).wait_send()
-
-
-def back(tok, gmid, query, keys, values, firsts, wqkv, gain, gmixed, lse, delta, cos, sine, nz):
+    if fused:
+        advance([last], "zero")
+        for j in jobs:
+            j.four()
+        for step in ("one", "two", "three"):
+            advance([last], step)
+        last.four()
+        for j in jobs + [last]:
+            j.done()
+    for k, device in ((0, me.twin), (1, me.beside), (2, me.twin)):
+        there(sent.at[k], landed.at[k], device, k).wait_send()
+
+    @pl.when(me.moves)
+    def _():
+        there(out_own, out, me.opposite, 3).wait()
+        there(gown, gtok, me.opposite, 4).wait()
+
+    @pl.when(me.stays)
+    def _():
+        here(out_own, out, 7).wait()
+        here(gown, gtok, 8).wait()
+
+
+def back(tok, gmid, out_own, query, keys, values, firsts, wqkv, gain, gmixed, lse, delta, cos, sine, packs, nz, masks):
     rows = tok.shape[0]
     shape, vm = jax.ShapeDtypeStruct, pltpu.VMEM
-    vmem = pl.BlockSpec(memory_space=pltpu.VMEM)
+    vmem, anyspace = pl.BlockSpec(memory_space=pltpu.VMEM), pl.BlockSpec(memory_space=pl.ANY)
+    in_specs = [vmem, vmem, anyspace, vmem, anyspace, anyspace, anyspace, anyspace] + [vmem] * 6
+    slab = (2 * SLIVER, 1280)
+    outs, out_specs = [shape((rows, WIDTH), BF)] * 2, [anyspace] * 2
+    scratch = [vm((2, rows, WIDTH), BF)] * 3 + [
+        vm((WIDTH, rows), BF),
+        vm((WIDTH, 3 * WIDTH), BF),
+        vm((WIDTH, rows), F32),
+        vm((rows, 2 * WIDTH), BF),
+        vm((rows, WIDTH), F32),
+        vm((WIDTH, 3 * WIDTH), F32),
+        vm((3, rows, WIDTH), BF),
+        vm((3, rows, WIDTH), BF),
+        vm((rows, WIDTH), BF),
+        vm((WIDTH, 128), F32),
+        pltpu.SemaphoreType.DMA((5,)),
+        pltpu.SemaphoreType.DMA((5,)),
+        pltpu.SemaphoreType.DMA((9,)),
+    ]
+    if masks:
+        in_specs += [anyspace] * 2
+        outs += [shape(s, F32) for s in (slab, packs[0].shape[-2:], packs[1].shape[-2:])]
+        out_specs += [vmem] * 3
+        scratch += [vm((GROUPS, LINE) + slab, BF)]
+        for s, held in ((slab, True), (packs[0].shape[-2:], False), (packs[1].shape[-2:], False)):
+            bufs, sems = Reduce.scratch(s, nz, held)
+            scratch += bufs + sems
+    else:
+        outs += [shape((GROUPS, LINE) + slab, BF)]
+        out_specs += [vmem]
+        packs = []
     return pl.pallas_call(
-        functools.partial(back_kernel, nz, rows),
-        out_shape=[shape((rows, WIDTH), BF), shape((GROUPS, LINE, 2 * SLIVER, 1280), BF)],
-        in_specs=[vmem] * 13,
-        out_specs=[vmem] * 2,
-        scratch_shapes=[
-            vm((WIDTH, rows), F32),
-            vm((rows, 2 * WIDTH), BF),
-            vm((rows, WIDTH), F32),
-            vm((WIDTH, 3 * WIDTH), F32),
-            vm((nz - 1, rows, WIDTH), BF),
-            vm((nz - 1, rows, WIDTH), BF),
-            vm((WIDTH, 128), F32),
-            pltpu.SemaphoreType.DMA((nz - 1,)),
-            pltpu.SemaphoreType.DMA((nz - 1,)),
-        ],
-        compiler_params=pltpu.CompilerParams(collective_id=1, has_side_effects=True, vmem_limit_bytes=58 << 20),
+        functools.partial(back_kernel, nz, masks, rows),
+        out_shape=outs,
+        in_specs=in_specs,
+        out_specs=out_specs,
+        scratch_shapes=scratch,
+        compiler_params=pltpu.CompilerParams(collective_id=1, has_side_effects=True, vmem_limit_bytes=60 << 20),
         cost_estimate=pl.CostEstimate(flops=24_000_000_000, bytes_accessed=40_000_000, transcendentals=13_000_000),
         name="back",
-    )(tok, gmid, query, keys, values, firsts, wqkv, gain, gmixed, lse, delta, cos, sine)
-
-
-class Reduce:
-    COPIES = 10
-
-    def __init__(self, src, total, cut, nz, masks, bufs, send, recv, loc):
-        self.src, self.total, self.cut, self.nz, self.masks = src, total, cut, nz, masks
-        self.mine, self.near, self.side0, self.side1, self.far = bufs
-        self.send, self.recv, self.loc = send, recv, loc
-        self.dp, self.z = lax.axis_index("dp"), lax.axis_index("seq")
-        my, mx, mc = masks
-        self.turns = (0, my, mx, my ^ mx)
-        self.started = []
-
-    @staticmethod
-    def scratch(shape, cut, nz):
-        r, c = shape
-        return [
-            pltpu.VMEM((4, nz, r, c), BF),
-            pltpu.VMEM((4, nz, r, c), BF),
-            pltpu.VMEM((3, nz, r, cut), BF),
-            pltpu.VMEM((3, nz, r, c - cut), BF),
-            pltpu.VMEM((nz - 1, r, c), BF),
-        ], [
-            pltpu.SemaphoreType.DMA((Reduce.COPIES * nz + nz,)),
-            pltpu.SemaphoreType.DMA((Reduce.COPIES * nz + nz,)),
-            pltpu.SemaphoreType.DMA((4 * nz,)),
-        ]
-
-    def begin(self, src, dst, device, k):
-        c = remote(src, dst, self.send.at[k], self.recv.at[k], device)
-        c.start()
-        self.started.append(c)
-
-    def arrived(self, ref, k):
-        remote(ref, ref, self.send.at[k], self.recv.at[k], {"dp": self.dp ^ self.masks[2]}).wait_recv()
-
-    def seat(self, o):
-        return lax.rem(self.z + o, self.nz)
-
-    def local(self, i, o):
-        s = self.seat(o)
-        return pltpu.make_async_copy(self.src.at[self.dp ^ self.turns[i], s], self.mine.at[i, s], self.loc.at[4 * o + i])
-
-    def zero(self, o):
-        s, mc = self.seat(o), self.masks[2]
-        for i in (3, 1, 2, 0):
-            self.local(i, o).start()
-            self.begin(self.src.at[self.dp ^ mc ^ self.turns[i], s], self.near.at[i, s], {"dp": self.dp ^ mc}, self.COPIES * o + i)
-
-    def add(self, ref, other):
-        ref[...] = (ref[...].astype(F32) + other[...].astype(F32)).astype(BF)
-
-    def p0(self, i, s):
-        return self.mine.at[i, s, :, pl.ds(0, self.cut)]
-
-    def p1(self, i, s):
-        return self.mine.at[i, s, :, pl.ds(self.cut, self.mine.shape[-1] - self.cut)]
-
-    def one(self, o):
-        my, mx, _ = self.masks
-        s, k = self.seat(o), self.COPIES * o
-        for i in (3, 1, 2, 0):
-            self.local(i, o).wait()
-            self.arrived(self.near.at[i, s], k + i)
-            self.add(self.mine.at[i, s], self.near.at[i, s])
-            if i == 3:
-                self.begin(self.p0(3, s), self.side0.at[1, s], {"dp": self.dp ^ my}, k + 4)
-                self.begin(self.p1(3, s), self.side1.at[1, s], {"dp": self.dp ^ mx}, k + 5)
-            if i == 1:
-                self.begin(self.p0(1, s), self.side0.at[0, s], {"dp": self.dp ^ my}, k + 6)
-            if i == 2:
-                self.begin(self.p1(2, s), self.side1.at[0, s], {"dp": self.dp ^ mx}, k + 7)
-
-    def two(self, o):
-        my, mx, _ = self.masks
-        s, k = self.seat(o), self.COPIES * o
-        self.arrived(self.side0.at[1, s], k + 4)
-        self.add(self.p0(2, s), self.side0.at[1, s])
-        self.begin(self.p0(2, s), self.side0.at[2, s], {"dp": self.dp ^ mx}, k + 8)
-        self.arrived(self.side1.at[1, s], k + 5)
-        self.add(self.p1(1, s), self.side1.at[1, s])
-        self.begin(self.p1(1, s), self.side1.at[2, s], {"dp": self.dp ^ my}, k + 9)
-
-    def three(self, o):
-        s, k = self.seat(o), self.COPIES * o
-        for ref, side, k1, k2 in ((self.p0(0, s), self.side0, k + 6, k + 8), (self.p1(0, s), self.side1, k + 7, k + 9)):
-            self.arrived(side.at[0, s], k1)
-            self.arrived(side.at[2, s], k2)
-            ref[...] = (ref[...].astype(F32) + side[0, s].astype(F32) + side[2, s].astype(F32)).astype(BF)
-        if o:
-            self.begin(self.mine.at[0, s], self.far.at[o - 1], {"seq": s}, self.COPIES * self.nz + o)
-
-    def four(self):
-        out = self.mine[0, self.z].astype(F32)
-        for o in range(1, self.nz):
-            self.arrived(self.far.at[o - 1], self.COPIES * self.nz + o)
-            out = out + self.far[o - 1].astype(F32)
-        self.total[...] = out
-
-    def done(self):
-        for c in self.started:
-            c.wait_send()
-
-
-def reduce_kernel(nz, masks, n, *refs):
-    srcs, totals, rest = refs[:n], refs[n : 2 * n], refs[2 * n :]
-    dp, z = lax.axis_index("dp"), lax.axis_index("seq")
-    greet(z, nz, dp, masks)
-    jobs = []
-    for i in range(n):
-        part = rest[8 * i : 8 * i + 8]
-        jobs.append(Reduce(srcs[i], totals[i], half_lanes(srcs[i].shape[-1]), nz, masks, part[:5], *part[5:]))
-    order = list(range(1, nz)) + [0]
-    for step in ("zero", "one", "two", "three"):
-        for j in jobs:
-            for o in order:
-                getattr(j, step)(o)
-    for j in jobs:
-        j.four()
-    for j in jobs:
-        j.done()
-
-
-def reduced(packs, nz, masks):
-    scratch = []
-    for p in packs:
-        bufs, sems = Reduce.scratch(p.shape[-2:], half_lanes(p.shape[-1]), nz)
-        scratch += bufs + sems
-    return pl.pallas_call(
-        functools.partial(reduce_kernel, nz, masks, len(packs)),
-        out_shape=[jax.ShapeDtypeStruct(p.shape[-2:], F32) for p in packs],
-        in_specs=[pl.BlockSpec(memory_space=pl.ANY)] * len(packs),
-        out_specs=[pl.BlockSpec(memory_space=pltpu.VMEM)] * len(packs),
-        scratch_shapes=scratch,
-        compiler_params=pltpu.CompilerParams(collective_id=2, has_side_effects=True, vmem_limit_bytes=58 << 20),
-        name="sum_packs",
-    )(*packs)
+    )(tok, gmid, out_own, query, keys, values, firsts, wqkv, gain, gmixed, lse, delta, cos, sine, *packs)
 
 
 def pack_qkv(w_qkv, gain):
@@ -912,19 +1024,24 @@
     cos, sine = [jnp.asarray(t).reshape(nz, rows, 128) for t in rope_tables(nz * rows)]
     if masks:
         packs = [pack_qkv(w_qkv, attn_gain), pack_out(w_out, mlp_gain), pack_mlp(w_in, w_down)]
-        mixed, lse, query, keys, values, firsts, wqkv, gain, po_all, pm_all = front(tokens, packs, cos, sine, nz, masks)
+        got = front(tokens, grad_out, packs, cos, sine, nz, masks)
+        po_all, pm_all = got[-2:]
     else:
         pq_all, po_all, pm_all = whole_packs(w_qkv, w_out, attn_gain, mlp_gain, w_in, w_down)
-        mixed, lse, query, keys, values, firsts, wqkv, gain = front(tokens, [pq_all], cos, sine, nz, None)
-    out, gmid, gmixed, delta, po_g, pm_g = middle(tokens, mixed, grad_out, po_all, pm_all)
-    gtok, pq_g = back(tokens, gmid, query, keys, values, firsts, wqkv, gain, gmixed, lse, delta, cos, sine, nz)
+        got = front(tokens, grad_out, [pq_all], cos, sine, nz, None)
+    mixed, lse, query, gain, tok_own, gout_own, keys, values, firsts, wqkv = got[:10]
+    out_own, gmid, gmixed, delta, po_g, pm_g = middle(tok_own, mixed, gout_own, po_all, pm_all)
+    found = back(
+        tok_own, gmid, out_own, query, keys, values, firsts, wqkv, gain, gmixed, lse, delta, cos, sine, [po_g, pm_g], nz, masks
+    )
+    gtok, out = found[:2]
     if masks:
-        sq, so, sm = reduced([pq_g, po_g, pm_g], nz, masks)
+        sq, so, sm = found[2:]
         g_qkv, g_gain_a = unpack_rows(sq)
         g_out, g_gain_m = unpack_rows(so)
         g_in, g_down = unpack_mlp(sm)
     else:
-        g_qkv, g_gain_a, g_out, g_gain_m, g_in, g_down = whole_sums(pq_g, po_g, pm_g)
+        g_qkv, g_gain_a, g_out, g_gain_m, g_in, g_down = whole_sums(found[2], po_g, pm_g)
     return out, gtok, g_qkv, g_out, g_gain_a, g_gain_m, g_in, g_down
 
 

time: 356 us -> 254 us (0.71)
  Pallas kernels: 336 us -> 233 us
    pallas_call x2 -> x1, Pallas kernels: 167 us -> 107 us  [back(): pl.pallas_call(functools.partial(back_kernel, nz, masks, rows), out_shape...]
    pallas_call x1, Pallas kernels: 141 us -> 97.9 us  [front(): pl.pallas_call(functools.partial(front_kernel, nz, masks, rows), out_shap...]
where the time goes in v2:
time: 254 us; the launch traced here: 253 us
  Pallas kernels  233 us (92%)
  local copies, waits for them, and re-layouts  16.2 us (6%)
  other arithmetic  2.69 us (1%)
    pallas_call x1, Pallas kernels, back(): pl.pallas_call(functools.partial(back_kernel, nz, masks, rows), out_shape...  107 us
    pallas_call x1, Pallas kernels, front(): pl.pallas_call(functools.partial(front_kernel, nz, masks, rows), out_shap...  97.9 us
    pallas_call x1, Pallas kernels, middle(): pl.pallas_call(functools.partial(middle_kernel, rows), out_shape=[shape((...  28.2 us

profile of v2, /device:TPU:0, one launch (start us, length us, event | category | flops | bytes accessed | tf_op | source)
XLA Modules:
  0.0 253.1 jit_solution(6068408505738876484)
XLA Ops:
  0.6 0.7 copy.25
  1.4 0.7 copy.26
  2.1 0.7 fusion.10
  2.9 0.6 fusion.3.refs_3_
  3.5 1.0 copy.29
  4.5 0.9 fusion.8
  5.4 0.7 fusion.1.refs_2_
  6.0 1.2 fusion.7
  7.4 0.8 concatenate.34.refs_4_
  8.2 97.9 %front.1 = (bf16[512,768]{1,0:T(8,128)(2,1)}, f32[16,512]{1,0:T(8,128)}, bf16[512,768]{1,0:T(8,128)(2,1)}, f32[8,768]{1,0:T(8,128)}, bf16[512,768]{1,0:T(8,128)(...) custom-call(bf16[512,768]{1,0:T(8,128)(2,1)} %refs_0_.1, ...), custom_call_target="tpu_custom_call" | custom-call | flops 14000000000 | bytes 40000000 | tf_op jit(solution)/shard_map/front/pallas_call | solution.py:442
  106.0 28.2 %middle.1 = (bf16[512,768]{1,0:T(8,128)(2,1)}, f32[512,768]{1,0:T(8,128)}, bf16[512,768]{1,0:T(8,128)(2,1)}, f32[16,512]{1,0:T(8,128)}, bf16[8,4,48,512]{3,2,1,0...) custom-call(bf16[512,768]{1,0:T(8,128)(2,1)} %get-tuple-element.31.tok.refs_0_, bf16[512,768]{1,0:T(8,128)(2,1)} %get-tuple-element.32.mixed, ...), custom_call_target="tpu_custom_call" | custom-call | flops 11000000512 | bytes 25000000 | tf_op jit(solution)/shard_map/middle/pallas_call | solution.py:575
  134.2 107.4 %back.1 = (bf16[512,768]{1,0:T(8,128)(2,1)}, bf16[512,768]{1,0:T(8,128)(2,1)}, f32[48,1280]{1,0:T(8,128)}, f32[48,512]{1,0:T(8,128)}, f32[96,896]{1,0:T(8,128)}) custom-call(bf16[512,768]{1,0:T(8,128)(2,1)} %get-tuple-element.31.tok.refs_0_, f32[512,768]{1,0:T(8,128)} %get-tuple-element.36.refs_1_, bf16[512,768]{1,0:T(8,128)(2,1)} %get-tuple-element.37.refs_2_, ...), custom_call_target="tpu_custom_call" | custom-call | flops 24000000000 | bytes 40000000 | tf_op jit(solution)/shard_map/back/pallas_call | solution.py:951
  241.6 0.0 copy-start.1
  241.6 0.0 copy-start
  241.6 1.4 slice_reduce_fusion.1
  243.0 1.0 fusion.6
  244.0 0.7 pad_maximum_fusion.1
  244.7 1.3 slice_reduce_fusion
  246.0 0.8 fusion.9
  246.8 0.6 pad_maximum_fusion.2
  247.5 1.0 fusion.5
  248.5 1.0 fusion.4
  249.5 0.8 copy.31
  250.4 0.9 copy.30
  251.3 0.0 copy-done.1
  251.3 0.9 copy.38
  252.2 0.0 copy-done
  252.2 0.9 copy.39
  (12 shorter events, 0.1 us)
Async XLA Ops:
  241.6 9.7 %copy-start.1 = (bf16[512,768]{1,0:T(8,128)(2,1)S(1)}, bf16[512,768]{1,0:T(8,128)(2,1)}, u32[]{:S(2)}) copy-start(bf16[512,768]{1,0:T(8,128)(2,1)} %get-tuple-element.96) | copy-start | bytes 2359300
  241.6 10.6 %copy-start = (bf16[512,768]{1,0:T(8,128)(2,1)S(1)}, bf16[512,768]{1,0:T(8,128)(2,1)}, u32[]{:S(2)}) copy-start(bf16[512,768]{1,0:T(8,128)(2,1)} %get-tuple-element.97) | copy-start | bytes 2359300

commit v3 on v2

--- a/solution.py
+++ b/solution.py
@@ -31,6 +31,9 @@
 SHARE = UNITS // LINE
 MAIN = 256
 REST = SHARE - MAIN
+LINKED = (0, 1, 3, 2)
+HALF = WIDTH // 2
+CUTS = {640: 256, 512: 256, 896: 384}
 LOG2E = math.log2(math.e)
 SCALE = HEAD_DIM**-0.5
 
@@ -120,6 +123,7 @@
         self.send, self.recv = send, recv
         self.dp, self.z = lax.axis_index("dp"), lax.axis_index("seq")
         self.started = []
+        self.relayed = None
 
     @staticmethod
     def sems(nz):
@@ -139,7 +143,7 @@
         self.copy(ref, ref, {"dp": self.dp ^ self.masks[0]}, k).wait_recv()
 
     def slot(self, o):
-        return lax.rem(self.z + self.nz - o, self.nz)
+        return self.z ^ LINKED[o]
 
     def part(self, ref, p):
         if p is None:
@@ -147,10 +151,14 @@
         width = self.out.shape[-1]
         return ref.at[:, pl.ds(0, self.cut)] if p == 0 else ref.at[:, pl.ds(self.cut, width - self.cut)]
 
-    def along(self):
-        for o in range(1, self.nz):
-            k = self.COPIES * self.nz + o
-            self.begin(self.src, self.out.at[self.dp, self.z], {"seq": lax.rem(self.z + o, self.nz)}, k)
+    def along(self, o):
+        self.begin(self.src, self.out.at[self.dp, self.z], {"seq": self.z ^ LINKED[o]}, self.COPIES * self.nz + o)
+
+    def relay(self, o):
+        ref = self.out.at[self.dp, self.slot(o)]
+        self.arrived(ref, self.COPIES * self.nz + o)
+        self.relayed = o
+        self.begin(ref, ref, {"seq": self.z ^ 1}, self.COPIES * self.nz + 3)
 
     def forward(self, src, d, s, mask, k, p=None):
         dst = self.out.at[d, s]
@@ -162,7 +170,8 @@
         src = self.src
         if o:
             src = self.out.at[self.dp, s]
-            self.arrived(src, self.COPIES * self.nz + o)
+            if o != self.relayed:
+                self.arrived(src, self.COPIES * self.nz + o)
         self.forward(src, self.dp, s, my, self.key(o, 0))
         self.forward(src, self.dp, s, mx, self.key(o, 1))
         self.forward(src, self.dp, s, mc, self.key(o, 2))
@@ -199,18 +208,44 @@
             self.copy(ref, ref, {"dp": self.dp ^ self.masks[0]}, k).wait_send()
 
 
-def half_lanes(width):
-    return (width // 256) * 128
+def pack_group(w, tile, i):
+    q, k, v = [w[:, WIDTH * j + HALF * i : WIDTH * j + HALF * i + HALF] for j in range(3)]
+    return jnp.concatenate([jnp.concatenate([q, v[:, :256]], 1), jnp.concatenate([k, v[:, 256:], tile], 1)], 0)
+
+
+def unpack_group(total):
+    r = total.shape[0] // 2
+    upper, lower = total[:r], total[r:]
+    return upper[:, :HALF], lower[:, :HALF], upper[:, HALF:], lower[:, HALF : HALF + 128], lower[:, HALF + 128 :]
+
+
+def pack_out(w, tile):
+    return jnp.concatenate([jnp.concatenate([w[:, :HALF], w[:, HALF:]], 0), jnp.concatenate([tile, jnp.zeros_like(tile)], 0)], 1)
+
+
+def pack_mlp(gate, up, down):
+    parts = (gate, up, down)
+    pads = jnp.zeros((gate.shape[0], 128 - 3 * REST), gate.dtype)
+    return jnp.concatenate([x[:, :MAIN] for x in parts] + [x[:, MAIN:] for x in parts] + [pads], 1)
+
+
+def unpack_mlp(total):
+    return [
+        jnp.concatenate([total[:, MAIN * i : MAIN * i + MAIN], total[:, 3 * MAIN + REST * i : 3 * MAIN + REST * i + REST]], 1)
+        for i in range(3)
+    ]
 
 
 def front_kernel(nz, masks, rows, *refs):
     fused = masks is not None
     if fused:
-        (tok, gout, pq, po, pm, cos, sine, mixed, lse, query, gain, tok_own, gout_own, keys, values, firsts, wqkv, po_all, pm_all,
-         tok_all, kb, vb, fb, wq, gcol, acc, top, total, tsend, trecv, loc, pq_all, qs, qr, os_, or_, ms, mr) = refs
+        (tok, gout, w_qkv, w_out, gains, w_in, w_down, cos_in, sine_in), refs = refs[:9], refs[9:]
     else:
-        (tok, gout, pq_all, cos, sine, mixed, lse, query, gain, tok_own, gout_own, keys, values, firsts, wqkv,
-         tok_all, kb, vb, fb, wq, gcol, acc, top, total, tsend, trecv, loc) = refs
+        (tok, gout, g0_all, g1_all, cos_in, sine_in), refs = refs[:6], refs[6:]
+    (mixed, lse, query, gain, tok_own, gout_own, kv, firsts, wqkv), refs = refs[:9], refs[9:]
+    if fused:
+        (po_all, pm_all), refs = refs[:2], refs[2:]
+    (tok_all, kvb, fb, wq, cos, sine, gcol, acc, top, total, tsend, trecv, loc), refs = refs[:13], refs[13:]
     me = Place(nz)
     own = me.shard
 
@@ -225,20 +260,29 @@
         here(tok, tok_all.at[own], 0).start()
         here(gout, gout_own, 1).start()
 
+    here(cos_in, cos, 2).start()
+    here(sine_in, sine, 3).start()
+    groups, later = [], []
+    every, rest = range(nz), (2, 1, 3)
     if fused:
-        locals_ = [here(src, out.at[me.dp, me.z], 2 + i) for i, (src, out) in enumerate(((pq, pq_all), (po, po_all), (pm, pm_all)))]
-        for c in locals_:
-            c.start()
+        p0, p1, po, pm, g0_all, g1_all, *sems = refs
+        row = lax.broadcasted_iota(jnp.int32, (128, 128), 0)
+
+        def tile_of(i):
+            return jnp.where(row == 0, gains[i : i + 1, :], 0.0).T[:SLIVER]
+
+        p0[...] = pack_group(w_qkv[...].astype(F32), tile_of(0), 0).astype(BF)
+        g0_all[me.dp, me.z] = p0[...]
     me.greet(masks or (1,))
     if fused:
+        shapes = ((p0, g0_all), (p1, g1_all), (po, po_all), (pm, pm_all))
         packs = [
-            Gather(pq, pq_all, half_lanes(pq.shape[-1]), nz, masks, qs, qr),
-            Gather(po, po_all, half_lanes(po.shape[-1]), nz, masks, os_, or_),
-            Gather(pm, pm_all, half_lanes(pm.shape[-1]), nz, masks, ms, mr),
+            Gather(src, dst, CUTS[src.shape[-1]], nz, masks, sems[2 * i], sems[2 * i + 1]) for i, (src, dst) in enumerate(shapes)
         ]
-        first, *later = packs
-        first.along()
-        first.first(0)
+        groups, later = packs[:2], packs[2:]
+        for o in rest:
+            groups[0].along(o)
+        groups[0].first(0)
 
     @pl.when(me.stays)
     def _():
@@ -250,47 +294,69 @@
         there(tok, tok_all.at[me.z], me.opposite, 0).start()
 
     if fused:
-        first.second(0)
-        for o in range(1, nz):
-            first.first(o)
-        for o in range(1, nz):
-            first.second(o)
-        for o in range(nz):
-            first.third(o)
+        w = w_qkv[...].astype(F32)
+        p1[...] = pack_group(w, jnp.zeros((SLIVER, 128), F32), 1).astype(BF)
+        g1_all[me.dp, me.z] = p1[...]
+        po[...] = pack_out(w_out[...].astype(F32), tile_of(1)).astype(BF)
+        w = w_in[...].astype(F32)
+        pm[...] = pack_mlp(w[:, :SHARE], w[:, SHARE:], w_down[...].astype(F32).T).astype(BF)
+        here(po, po_all.at[me.dp, me.z], 4).start()
+        here(pm, pm_all.at[me.dp, me.z], 5).start()
+        for o in rest:
+            groups[1].along(o)
+        groups[1].first(0)
+        groups[0].second(0)
+        for o in rest:
+            groups[0].first(o)
+        for o in rest:
+            groups[0].second(o)
+        for o in rest:
+            groups[1].first(o)
+        for g in later:
+            g.along(1)
+            g.first(0)
 
     @pl.when(me.moves)
     def _():
         there(tok, tok_all.at[own], me.opposite, 0).wait_recv()
         there(tok_all.at[own], tok_all.at[own], me.twin, 1).start()
         there(tok_all.at[own], tok_all.at[own], me.beside, 2).start()
-        there(gout, gout_own, me.opposite, 4).start()
 
     @pl.when(me.stays)
     def _():
         here(tok, tok_all.at[own], 0).wait()
 
-    here(tok_all.at[own], tok_own, 5).start()
+    here(tok_all.at[own], tok_own, 6).start()
     if fused:
         for g in later:
-            g.along()
-            g.first(0)
-        locals_[0].wait()
+            g.along(2)
         for o in range(nz):
-            first.finish(o)
-
-    half = 1152
-
-    def build(g, _):
-        slabs = [pq_all[g, s].astype(F32) for s in range(LINE)]
-        band = pl.ds(pl.multiple_of(g * BAND, BAND), BAND)
-        wq[band, :half] = jnp.concatenate([x[:SLIVER, :half] for x in slabs], 0).astype(BF)
-        wq[band, half:] = jnp.concatenate([x[SLIVER:, :half] for x in slabs], 0).astype(BF)
-        gcol[band, :] = jnp.concatenate([x[:SLIVER, half:] for x in slabs], 0)
-        return 0
-
-    lax.fori_loop(0, GROUPS, build, 0)
-    here(wq, wqkv, 6).start()
-    gain[...] = gcol[...].T[:8]
+            groups[0].third(o)
+        for o in range(nz):
+            groups[0].finish(o)
+
+    @pl.when(me.moves)
+    def _():
+        there(gout, gout_own, me.opposite, 4).start()
+
+    here(cos_in, cos, 2).wait()
+    here(sine_in, sine, 3).wait()
+
+    def build(i, whole):
+        def band_of(g, _):
+            slabs = [unpack_group(whole[g, s].astype(F32)) for s in range(LINE)]
+            band = pl.ds(pl.multiple_of(g * BAND, BAND), BAND)
+            q, k, v0, v1, t = [jnp.concatenate([x[j] for x in slabs], 0) for j in range(5)]
+            at = WIDTH * i
+            wq[band, at : at + HALF] = k.astype(BF)
+            wq[band, at + HALF : at + HALF + 256] = v0.astype(BF)
+            wq[band, at + HALF + 256 : at + WIDTH] = v1.astype(BF)
+            wq[band, 2 * WIDTH + HALF * i : 2 * WIDTH + HALF * i + HALF] = q.astype(BF)
+            if i == 0:
+                gcol[band, :] = t
+            return 0
+
+        lax.fori_loop(0, GROUPS, band_of, 0)
 
     def norm_chunk(c):
         def block(i, _):
@@ -300,83 +366,88 @@
             return 0
 
         lax.fori_loop(0, rows // 64, block, 0)
-        here(fb.at[c], firsts.at[c], 7 + c).start()
-
-    def project(c, j, base):
-        return dot(fb[c], wq[:, base + 256 * j : base + 256 * j + 256], NN)
-
+        here(fb.at[c], firsts.at[c], 8 + c).start()
+
+    def queries(i):
+        u = dot(fb[own], wq[:, 2 * WIDTH + HALF * i : 2 * WIDTH + HALF * i + HALF], NN)
+        for j in range(3):
+            tile = rope(u[:, 128 * j : 128 * j + 128], cos[own], sine[own])
+            query[:, HALF * i + 128 * j : HALF * i + 128 * j + 128] = (tile * (SCALE * LOG2E)).astype(BF)
+
+    def visits(grp, steps):
+        def visit(t, _):
+            c = jnp.where(t == 0, own, jnp.where(t == 1, own ^ 3, jnp.where(t == 2, own ^ 1, own ^ 2)))
+            if grp == 0:
+
+                @pl.when(t > 0)
+                def _():
+                    there(tok_all.at[c], tok_all.at[c], me.twin, t).wait_recv()
+
+                    @pl.when(t == 2)
+                    def _():
+                        there(tok_all.at[c], tok_all.at[c], me.twin, 3).start()
+
+                    norm_chunk(c)
+
+            for j in range(3):
+                u = dot(fb[c], wq[:, WIDTH * grp + 256 * j : WIDTH * grp + 256 * j + 256], NN)
+                for i in range(2):
+                    n = 2 * j + i
+                    x = u[:, 128 * i : 128 * i + 128]
+                    x = rope(x, cos[c], sine[c]) if n < 3 else x
+                    kvb[grp, c, :, 128 * n : 128 * n + 128] = x.astype(BF)
+            here(kvb.at[grp, c], kv.at[grp, c], 8 + nz * (1 + grp) + c).start()
+            jobs = [(i, h) for i in range(3) for h in range(2)]
+
+            def score(i, h):
+                q = query[:, HALF * grp + 128 * i : HALF * grp + 128 * i + 128]
+                mask = (lane_iota() < 64) if h == 0 else (lane_iota() >= 64)
+                return dot(kvb[grp, c, :, 128 * i : 128 * i + 128], jnp.where(mask, q, jnp.zeros_like(q)), NT)
+
+            ready = [score(*j) for j in jobs[:2]]
+            for n, (i, h) in enumerate(jobs):
+                if h == 0:
+                    vt = kvb[grp, c, :, HALF + 128 * i : HALF + 128 * i + 128].T
+                s = ready[n]
+                if n + 2 < len(jobs):
+                    ready.append(score(*jobs[n + 2]))
+                head = 6 * grp + n
+                old = top[head : head + 1, :]
+                new = jnp.maximum(old, jnp.max(s, 0, keepdims=True))
+                p = jnp.exp2(s - new)
+                fade = jnp.exp2(old - new)
+                top[head : head + 1, :] = new
+                lhs = jnp.concatenate([vt[h * 64 : h * 64 + 64], jnp.ones((16, rows), BF)], 0)
+                oo = dot(lhs, p.astype(BF), NN)
+                total[head : head + 1, :] = total[head : head + 1, :] * fade + oo[64:65]
+                acc[64 * head : 64 * head + 64, :] = acc[64 * head : 64 * head + 64, :] * fade + oo[:64]
+            if fused:
+                for k, step in steps.items():
+
+                    @pl.when(t == k)
+                    def _(step=step):
+                        for which, name, order in step:
+                            for g in which:
+                                for o in order:
+                                    getattr(g, name)(o)
+
+            return 0
+
+        lax.fori_loop(0, nz, visit, 0)
+
+    build(0, g0_all)
+    gain[...] = gcol[...].T[:8]
     norm_chunk(own)
-    for j in range(3):
-        u = project(own, j, 0)
-        for i in range(2):
-            tile = rope(u[:, 128 * i : 128 * i + 128], cos[own], sine[own])
-            query[:, 256 * j + 128 * i : 256 * j + 128 * i + 128] = (tile * (SCALE * LOG2E)).astype(BF)
+    queries(0)
     acc[...] = jnp.zeros_like(acc)
     total[...] = jnp.zeros_like(total)
     top[...] = jnp.full_like(top, -1e30)
-
-    def visit(t, _):
-        c = jnp.where(t == 0, own, jnp.where(t == 1, own ^ 3, jnp.where(t == 2, own ^ 1, own ^ 2)))
-
-        @pl.when(t > 0)
-        def _():
-            there(tok_all.at[c], tok_all.at[c], me.twin, t).wait_recv()
-
-            @pl.when(t == 2)
-            def _():
-                there(tok_all.at[c], tok_all.at[c], me.twin, 3).start()
-
-            norm_chunk(c)
-
-        for j in range(3):
-            u = project(c, j, WIDTH)
-            for i in range(2):
-                at = 256 * j + 128 * i
-                kb[c, :, at : at + 128] = rope(u[:, 128 * i : 128 * i + 128], cos[c], sine[c]).astype(BF)
-            vb[c, :, 256 * j : 256 * j + 256] = project(c, j, 2 * WIDTH).astype(BF)
-        here(kb.at[c], keys.at[c], 7 + nz + c).start()
-        here(vb.at[c], values.at[c], 7 + 2 * nz + c).start()
-
-        def pair(hp, _):
-            q, k, v = query[:, lanes_of(hp)], kb[c, :, lanes_of(hp)], vb[c, :, lanes_of(hp)]
-            for h in range(2):
-                mask = (lane_iota() < 64) if h == 0 else (lane_iota() >= 64)
-                s = dot(k, jnp.where(mask, q, jnp.zeros_like(q)), NT)
-                at = pl.ds(hp * 2 + h, 1)
-                old = top[at, :]
-                new = jnp.maximum(old, jnp.max(s, 0, keepdims=True))
-                p = jnp.exp2(s - new)
-                fade = jnp.exp2(old - new)
-                top[at, :] = new
-                total[at, :] = total[at, :] * fade + jnp.sum(p, 0, keepdims=True)
-                band = pl.ds(pl.multiple_of(hp * 128 + h * 64, 64), 64)
-                acc[band, :] = acc[band, :] * fade + dot(v[:, h * 64 : h * 64 + 64], p.astype(BF), TN)
-            return 0
-
-        lax.fori_loop(0, PAIRS, pair, 0)
-        if fused:
-
-            @pl.when(t == 1)
-            def _():
-                for g in later:
-                    for o in range(1, nz):
-                        g.first(o)
-
-            @pl.when(t == 2)
-            def _():
-                for g in later:
-                    for o in range(nz):
-                        g.second(o)
-
-            @pl.when(t == 3)
-            def _():
-                for g in later:
-                    for o in range(nz):
-                        g.third(o)
-
-        return 0
-
-    lax.fori_loop(0, nz, visit, 0)
+    one = groups[1:]
+    visits(0, {0: [(one, "second", every), (later, "first", (1,))], 1: [(one, "third", every)], 2: [(later, "relay", (2,)), (later, "first", (2,))], 3: [(one, "finish", every), (later, "second", (0, 1))]})
+    build(1, g1_all)
+    here(wq, wqkv, 7).start()
+    queries(1)
+    visits(1, {0: [(later, "first", (3,))], 1: [(later, "second", (2,))], 2: [(later, "second", (3,))], 3: [(later, "third", every)]})
 
     for hp in range(PAIRS):
         parts = [
@@ -391,8 +462,8 @@
                 g.finish(o)
         for g in packs:
             g.done()
-        for c in locals_[1:]:
-            c.wait()
+        here(po, po_all.at[me.dp, me.z], 4).wait()
+        here(pm, pm_all.at[me.dp, me.z], 5).wait()
     there(tok, tok_all.at[own], me.twin, 1).wait_send()
     there(tok, tok_all.at[own], me.beside, 2).wait_send()
     there(tok_all.at[own], tok_all.at[own], me.twin, 3).wait_send()
@@ -406,49 +477,53 @@
     def _():
         here(gout, gout_own, 1).wait()
 
-    here(tok_all.at[own], tok_own, 5).wait()
-    here(wq, wqkv, 6).wait()
+    here(tok_all.at[own], tok_own, 6).wait()
+    here(wq, wqkv, 7).wait()
     for c in range(nz):
-        for i, (buf, dst) in enumerate(((fb, firsts), (kb, keys), (vb, values))):
-            here(buf.at[c], dst.at[c], 7 + nz * i + c).wait()
-
-
-def front(tok, gout, packs, cos, sine, nz, masks):
+        here(fb.at[c], firsts.at[c], 8 + c).wait()
+        for grp in range(2):
+            here(kvb.at[grp, c], kv.at[grp, c], 8 + nz * (1 + grp) + c).wait()
+
+
+def front(tok, gout, weights, cos, sine, nz, masks):
     rows = tok.shape[0]
-    fused = masks is not None
     vmem, anyspace = pl.BlockSpec(memory_space=pltpu.VMEM), pl.BlockSpec(memory_space=pl.ANY)
     shape, vm = jax.ShapeDtypeStruct, pltpu.VMEM
     outs = [shape((rows, WIDTH), BF), shape((16, rows), F32), shape((rows, WIDTH), BF), shape((8, WIDTH), F32)]
-    outs += [shape((rows, WIDTH), BF)] * 2 + [shape((nz, rows, WIDTH), BF)] * 3 + [shape((WIDTH, 3 * WIDTH), BF)]
-    out_specs = [vmem] * 4 + [anyspace] * 6
-    scratch = [vm((nz, rows, WIDTH), BF)] * 4 + [
+    outs += [shape((rows, WIDTH), BF)] * 2
+    outs += [shape((2, nz, rows, WIDTH), BF), shape((nz, rows, WIDTH), BF), shape((WIDTH, 3 * WIDTH), BF)]
+    out_specs = [vmem] * 4 + [anyspace, vmem] + [anyspace] * 3
+    scratch = [
+        vm((nz, rows, WIDTH), BF),
+        vm((2, nz, rows, WIDTH), BF),
+        vm((nz, rows, WIDTH), BF),
         vm((WIDTH, 3 * WIDTH), BF),
+        vm((nz, rows, 128), F32),
+        vm((nz, rows, 128), F32),
         vm((WIDTH, 128), F32),
         vm((WIDTH, rows), F32),
         vm((16, rows), F32),
         vm((16, rows), F32),
         pltpu.SemaphoreType.DMA((5,)),
         pltpu.SemaphoreType.DMA((5,)),
-        pltpu.SemaphoreType.DMA((7 + 3 * nz,)),
+        pltpu.SemaphoreType.DMA((8 + 3 * nz,)),
     ]
-    if fused:
-        pq, po, pm = packs
-        outs += [shape((GROUPS, nz) + po.shape, BF), shape((GROUPS, nz) + pm.shape, BF)]
+    if masks:
+        grp, out, mlp = (2 * SLIVER, 640), (2 * SLIVER, 512), (BAND, 896)
+        outs += [shape((GROUPS, nz) + out, BF), shape((GROUPS, nz) + mlp, BF)]
         out_specs += [anyspace] * 2
-        in_specs = [anyspace] * 5 + [vmem] * 2
-        scratch += [vm((GROUPS, nz) + pq.shape, BF)] + [pltpu.SemaphoreType.DMA((Gather.sems(nz),)) for _ in range(6)]
-    else:
-        in_specs = [anyspace] * 2 + [vmem] * 3
+        scratch += [vm(x, BF) for x in (grp, grp, out, mlp)] + [vm((GROUPS, nz) + grp, BF)] * 2
+        scratch += [pltpu.SemaphoreType.DMA((Gather.sems(nz),)) for _ in range(8)]
     return pl.pallas_call(
         functools.partial(front_kernel, nz, masks, rows),
         out_shape=outs,
-        in_specs=in_specs,
+        in_specs=[anyspace] * 2 + [vmem] * len(weights) + [anyspace] * 2,
         out_specs=out_specs,
         scratch_shapes=scratch,
-        compiler_params=pltpu.CompilerParams(collective_id=0, has_side_effects=True, vmem_limit_bytes=58 << 20),
+        compiler_params=pltpu.CompilerParams(collective_id=0, has_side_effects=True, vmem_limit_bytes=60 << 20),
         cost_estimate=pl.CostEstimate(flops=14_000_000_000, bytes_accessed=40_000_000, transcendentals=13_000_000),
         name="front",
-    )(tok, gout, *packs, cos, sine)
+    )(tok, gout, *weights, cos, sine)
 
 
 def middle_kernel(rows, tok, mixed, gout, po_all, pm_all, out, gmid, gmixed, delta, po_g, pm_g,
@@ -624,7 +699,7 @@
     @staticmethod
     def scratch(shape, nz, held):
         r, c = shape
-        cut = half_lanes(c)
+        cut = CUTS[c]
         bufs = [
             pltpu.VMEM((4, nz, r, c), BF),
             pltpu.VMEM((3, nz, r, cut), BF),
@@ -645,7 +720,7 @@
         remote(ref, ref, self.send.at[k], self.recv.at[k], {"dp": self.dp ^ self.masks[2]}).wait_recv()
 
     def seat(self, o):
-        return lax.rem(self.z + o, self.nz)
+        return self.z ^ LINKED[o]
 
     def held(self, i, s):
         return self.mine.at[i, s] if self.mine is not None else self.src.at[self.dp ^ self.turns[i], s]
@@ -721,15 +796,14 @@
 
 def back_kernel(nz, masks, rows, *refs):
     fused = masks is not None
-    (tok, gmid, out_own, query, keys, values, firsts, wqkv, gain, gmixed, lse, delta, cos, sine), refs = refs[:14], refs[14:]
+    (tok, gmid, out_own, query, kv, firsts, wqkv, gain, gmixed, lse, delta, cos_in, sine_in), refs = refs[:13], refs[13:]
     if fused:
-        (po_g, pm_g, gtok, out, sq, so, sm), refs = refs[:7], refs[7:]
+        (po_g, pm_g, gtok, out, s0, s1, so, sm), refs = refs[:8], refs[8:]
     else:
-        (gtok, out, pq_g), refs = refs[:3], refs[3:]
-    (kb, vb, fb, ft, wq, dq, dkv, dx, dw, sent, landed, gown, gcol, send, recv, loc), refs = refs[:16], refs[16:]
+        (gtok, out, p0_g, p1_g), refs = refs[:4], refs[4:]
+    (kvb, fb, ft, wq, cos, sine, dq, dqb, dkv, dx, dw, sent, landed, gown, gcol, send, recv, loc), refs = refs[:18], refs[18:]
     me = Place(nz)
     own = me.shard
-    me.greet(masks or (1,))
 
     def here(src, dst, k):
         return pltpu.make_async_copy(src, dst, loc.at[k])
@@ -740,28 +814,42 @@
     def chunk(t):
         return jnp.where(t == 0, own ^ 2, jnp.where(t == 1, own ^ 1, jnp.where(t == 2, own ^ 3, own)))
 
-    def fetch(t):
+    def fetch(grp, t):
         c, slot = chunk(t), lax.rem(t, 2)
-        return [here(src.at[c], buf.at[slot], 3 * slot + i) for i, (src, buf) in enumerate(((keys, kb), (values, vb), (firsts, fb)))]
-
-    for c in fetch(0):
+        found = [here(kv.at[grp, c], kvb.at[slot], slot)]
+        if grp == 0:
+            found.append(here(firsts.at[c], fb.at[slot], 2 + slot))
+        return found
+
+    for c in fetch(0, 0):
         c.start()
-    here(wqkv, wq, 6).start()
-    jobs = []
+    whole = [here(wqkv, wq, 4), here(cos_in, cos, 5), here(sine_in, sine, 6)]
+    for c in whole:
+        c.start()
+    me.greet(masks or (1,))
+    jobs, sums = [], []
     if fused:
-        pq_g, refs = refs[0], refs[1:]
-        last = Reduce(pq_g, sq, half_lanes(pq_g.shape[-1]), nz, masks, refs[:4], *refs[4:6])
-        refs = refs[6:]
+        (p0_g, p1_g), refs = refs[:2], refs[2:]
+        for src, total in ((p0_g, s0), (p1_g, s1)):
+            sums.append(Reduce(src, total, CUTS[src.shape[-1]], nz, masks, refs[:4], *refs[4:6]))
+            refs = refs[6:]
         for src, total in ((po_g, so), (pm_g, sm)):
-            jobs.append(Reduce(src, total, half_lanes(src.shape[-1]), nz, masks, refs[:5], *refs[5:8]))
+            jobs.append(Reduce(src, total, CUTS[src.shape[-1]], nz, masks, refs[:5], *refs[5:8]))
             refs = refs[8:]
-    order = list(range(1, nz)) + [0]
+    order = (3, 2, 1, 0)
 
     def advance(which, step):
         for j in which:
             for o in order:
                 getattr(j, step)(o)
 
+    def wave(which):
+        for i in range(nz + 2):
+            for k, step in enumerate(("one", "two", "three")):
+                if 0 <= i - k < nz:
+                    for j in which:
+                        getattr(j, step)(order[i - k])
+
     advance(jobs, "zero")
 
     @pl.when(me.moves)
@@ -773,92 +861,129 @@
         here(out_own, out, 7).start()
 
     dq[...] = jnp.zeros_like(dq)
-    dw[...] = jnp.zeros_like(dw)
-
-    def visit(t, _):
-        c, slot = chunk(t), lax.rem(t, 2)
-        for f in fetch(t):
-            f.wait()
-
-        @pl.when(t + 1 < nz)
-        def _():
-            for f in fetch(t + 1):
-                f.start()
-
-        def pair(hp, _):
-            at = lanes_of(hp)
-            q, g, k, v = query[:, at], gmixed[:, at], kb[slot, :, at], vb[slot, :, at]
+    for c in whole:
+        c.wait()
+
+    def visits(grp, steps):
+        def visit(t, _):
+            c, slot = chunk(t), lax.rem(t, 2)
+            for f in fetch(grp, t):
+                f.wait()
+
+            @pl.when(t + 1 < nz)
+            def _():
+                for f in fetch(grp, t + 1):
+                    f.start()
+
+            if grp == 0:
+
+                @pl.when(t + 1 == nz)
+                def _():
+                    for f in fetch(1, 0):
+                        f.start()
+
+            band = pl.ds(pl.multiple_of(t * rows, rows), rows)
+            todo = [(i, h) for i in range(3) for h in range(2)]
+
+            def pick(ref, i, h):
+                x = ref[:, HALF * grp + 128 * i : HALF * grp + 128 * i + 128]
+                mask = (lane_iota() < 64) if h == 0 else (lane_iota() >= 64)
+                return jnp.where(mask, x, jnp.zeros_like(x))
+
+            def score(i, h):
+                qh, gh = pick(query, i, h), pick(gmixed, i, h)
+                k, v = kvb[slot, :, 128 * i : 128 * i + 128], kvb[slot, :, HALF + 128 * i : HALF + 128 * i + 128]
+                return dot(k, qh, NT), dot(v, gh, NT), qh, gh
+
+            ready = [score(*todo[0])]
             dk = dv = None
-            for h in range(2):
-                mask = (lane_iota() < 64) if h == 0 else (lane_iota() >= 64)
-                qh, gh = jnp.where(mask, q, jnp.zeros_like(q)), jnp.where(mask, g, jnp.zeros_like(g))
-                head = pl.ds(hp * 2 + h, 1)
-                p = jnp.exp2(dot(k, qh, NT) - lse[head, :])
-                ds = (p * (dot(v, gh, NT) - delta[head, :])).astype(BF)
+            for n, (i, h) in enumerate(todo):
+                s, dp, qh, gh = ready[n]
+                if n + 1 < len(todo):
+                    ready.append(score(*todo[n + 1]))
+                if h == 0:
+                    kt = kvb[slot, :, 128 * i : 128 * i + 128].T
+                head = 6 * grp + n
+                p = jnp.exp2(s - lse[head : head + 1, :])
+                ds = (p * (dp - delta[head : head + 1, :])).astype(BF)
                 a = dot(p.astype(BF), gh, NN)
-                dv = a if dv is None else dv + a
+                dv = a if h == 0 else dv + a
                 a = dot(ds, qh, NN)
-                dk = a if dk is None else dk + a
-                band = pl.ds(pl.multiple_of(hp * 128 + h * 64, 64), 64)
-                dq[band, :] += dot(k[:, h * 64 : h * 64 + 64], ds, TN)
-            dkv[:, at] = rope_back(dk * (1.0 / LOG2E), cos[c], sine[c]).astype(BF)
-            dkv[:, lanes_of(hp + PAIRS)] = dv.astype(BF)
+                dk = a if h == 0 else dk + a
+                dq[64 * head : 64 * head + 64, :] += dot(kt[h * 64 : h * 64 + 64], ds, NN)
+                if h == 1:
+                    at = WIDTH * grp + 128 * i
+                    dkv[band, at : at + 128] = rope_back(dk * (1.0 / LOG2E), cos[c], sine[c]).astype(BF)
+                    dkv[band, at + HALF : at + HALF + 128] = dv.astype(BF)
+
+            if grp == 0:
+                for j in range(6):
+                    ft[128 * j : 128 * j + 128, band] = fb[slot, :, 128 * j : 128 * j + 128].T
+            else:
+                for j in range(3):
+                    at = slice(256 * j, 256 * j + 256)
+                    dx[:, at] = dot(dkv[band, :], wq[at, : 2 * WIDTH], NT)
+
+                @pl.when(lax.rem(t, 2) == 0)
+                def _():
+                    sent[t] = dx[...].astype(BF)
+                    there(sent.at[t], landed.at[t], me.twin, t).start()
+
+                @pl.when(t == 1)
+                def _():
+                    there(sent.at[0], landed.at[0], me.twin, 0).wait_recv()
+                    sent[1] = (dx[...] + landed[0].astype(F32)).astype(BF)
+                    there(sent.at[1], landed.at[1], me.beside, 1).start()
+
+            if fused:
+                for k, step in steps.items():
+
+                    @pl.when(t == k)
+                    def _(step=step):
+                        for which, name in step:
+                            if name == "four":
+                                for j in which:
+                                    j.four()
+                            else:
+                                advance(which, name)
+
             return 0
 
-        lax.fori_loop(0, PAIRS, pair, 0)
-
-        @pl.when(t == 0)
-        def _():
-            here(wqkv, wq, 6).wait()
-
-        for j in range(3):
-            at = slice(256 * j, 256 * j + 256)
-            dx[:, at] = dot(dkv[...], wq[at, WIDTH:], NT)
-
-        @pl.when(lax.rem(t, 2) == 0)
-        def _():
-            sent[t] = dx[...].astype(BF)
-            there(sent.at[t], landed.at[t], me.twin, t).start()
-
-        @pl.when(t == 1)
-        def _():
-            there(sent.at[0], landed.at[0], me.twin, 0).wait_recv()
-            sent[1] = (dx[...] + landed[0].astype(F32)).astype(BF)
-            there(sent.at[1], landed.at[1], me.beside, 1).start()
-
-        for j in range(6):
-            ft[128 * j : 128 * j + 128, :] = fb[slot, :, 128 * j : 128 * j + 128].T
-
-        def weigh(i, _):
-            at, to = lanes_of(i, 256), lanes_of(i + 3, 256)
-            for j in range(2):
-                r = slice(384 * j, 384 * j + 384)
-                dw[r, to] += dot(ft[r, :], dkv[:, at], NN)
+        lax.fori_loop(0, nz, visit, 0)
+        for i in range(3 * grp, 3 * grp + 3):
+            at = slice(128 * i, 128 * i + 128)
+            dqb[:, at] = rope_back(dq[at, :].T * SCALE, cos[own], sine[own]).astype(BF)
+
+    def weigh(grp):
+        for r in (slice(0, HALF), slice(HALF, WIDTH)):
+            for j in range(3):
+                at = WIDTH * grp + 256 * j
+                dw[r, HALF + 256 * j : HALF + 256 * j + 256] = dot(ft[r, :], dkv[:, at : at + 256], NN)
+            dw[r, :HALF] = dot(ft[r, (nz - 1) * rows :], dqb[:, HALF * grp : HALF * grp + HALF], NN)
+
+    def pack(grp, dst):
+        def band_of(g, _):
+            for s in range(LINE):
+                at = pl.ds(pl.multiple_of(g * BAND + s * SLIVER, 8), SLIVER)
+                q, k, v0, v1 = dw[at, :HALF], dw[at, HALF:WIDTH], dw[at, WIDTH : WIDTH + 256], dw[at, WIDTH + 256 :]
+                tile = gcol[at, :] if grp else jnp.zeros((SLIVER, 128), F32)
+                dst[g, s] = jnp.concatenate(
+                    [jnp.concatenate([q, v0], 1), jnp.concatenate([k, v1, tile], 1)], 0
+                ).astype(BF)
             return 0
 
-        lax.fori_loop(0, 6, weigh, 0)
-        if fused:
-            for k, step in enumerate(("one", "two", "three")):
-
-                @pl.when(t == k)
-                def _(step=step):
-                    advance(jobs, step)
-
-        return 0
-
-    lax.fori_loop(0, nz, visit, 0)
-
-    for hp in range(PAIRS):
-        at = slice(128 * hp, 128 * hp + 128)
-        u = dq[at, :].T * SCALE
-        dkv[:, at] = rope_back(u, cos[own], sine[own]).astype(BF)
+        lax.fori_loop(0, GROUPS, band_of, 0)
+
+    visits(0, {0: [(jobs, "one")]})
+    weigh(0)
+    pack(0, p0_g)
+    early = sums[:1]
+    advance(early, "zero")
+    visits(1, {0: [(jobs, "two"), (early, "one")], 2: [(jobs, "three")], 3: [(early, "two"), (early, "three")]})
     for j in range(3):
         at = slice(256 * j, 256 * j + 256)
-        dx[:, at] += dot(dkv[:, :WIDTH], wq[at, :WIDTH], NT)
-        for i in range(2):
-            r = slice(384 * i, 384 * i + 384)
-            dw[r, at] = dot(ft[r, :], dkv[:, at], NN)
-
+        dx[:, at] += dot(dqb[...], wq[at, 2 * WIDTH :], NT)
+    weigh(1)
     there(sent.at[1], landed.at[1], me.beside, 1).wait_recv()
     there(sent.at[2], landed.at[2], me.twin, 2).wait_recv()
 
@@ -881,24 +1006,14 @@
 
     row = lax.broadcasted_iota(jnp.int32, (128, WIDTH), 0)
     gcol[...] = jnp.where(row == 0, dgain, 0.0).T
-
-    def pack(g, _):
-        for s in range(LINE):
-            at = pl.ds(pl.multiple_of(g * BAND + s * SLIVER, 8), SLIVER)
-            x, c = dw[at, :], gcol[at, :]
-            pq_g[g, s, :, :1152] = jnp.concatenate([x[:, :1152], x[:, 1152:]], 0).astype(BF)
-            pq_g[g, s, :, 1152:] = jnp.concatenate([c, jnp.zeros_like(c)], 0).astype(BF)
-        return 0
-
-    lax.fori_loop(0, GROUPS, pack, 0)
+    pack(1, p1_g)
     if fused:
-        advance([last], "zero")
-        for j in jobs:
+        advance(sums[1:], "zero")
+        for j in jobs + early:
             j.four()
-        for step in ("one", "two", "three"):
-            advance([last], step)
-        last.four()
-        for j in jobs + [last]:
+        wave(sums[1:])
+        sums[1].four()
+        for j in jobs + sums:
             j.done()
     for k, device in ((0, me.twin), (1, me.beside), (2, me.twin)):
         there(sent.at[k], landed.at[k], device, k).wait_send()
@@ -914,20 +1029,25 @@
         here(gown, gtok, 8).wait()
 
 
-def back(tok, gmid, out_own, query, keys, values, firsts, wqkv, gain, gmixed, lse, delta, cos, sine, packs, nz, masks):
+def back(tok, gmid, out_own, query, kv, firsts, wqkv, gain, gmixed, lse, delta, cos, sine, packs, nz, masks):
     rows = tok.shape[0]
     shape, vm = jax.ShapeDtypeStruct, pltpu.VMEM
     vmem, anyspace = pl.BlockSpec(memory_space=pltpu.VMEM), pl.BlockSpec(memory_space=pl.ANY)
-    in_specs = [vmem, vmem, anyspace, vmem, anyspace, anyspace, anyspace, anyspace] + [vmem] * 6
-    slab = (2 * SLIVER, 1280)
-    outs, out_specs = [shape((rows, WIDTH), BF)] * 2, [anyspace] * 2
-    scratch = [vm((2, rows, WIDTH), BF)] * 3 + [
-        vm((WIDTH, rows), BF),
+    in_specs = [vmem] * 4 + [anyspace] * 3 + [vmem] * 4 + [anyspace] * 2
+    slab = (2 * SLIVER, 640)
+    outs, out_specs = [shape((rows, WIDTH), BF)] * 2, [vmem] * 2
+    scratch = [
+        vm((2, rows, WIDTH), BF),
+        vm((2, rows, WIDTH), BF),
+        vm((WIDTH, nz * rows), BF),
         vm((WIDTH, 3 * WIDTH), BF),
+        vm((nz, rows, 128), F32),
+        vm((nz, rows, 128), F32),
         vm((WIDTH, rows), F32),
-        vm((rows, 2 * WIDTH), BF),
+        vm((rows, WIDTH), BF),
+        vm((nz * rows, 2 * WIDTH), BF),
         vm((rows, WIDTH), F32),
-        vm((WIDTH, 3 * WIDTH), F32),
+        vm((WIDTH, 3 * HALF), F32),
         vm((3, rows, WIDTH), BF),
         vm((3, rows, WIDTH), BF),
         vm((rows, WIDTH), BF),
@@ -938,15 +1058,15 @@
     ]
     if masks:
         in_specs += [anyspace] * 2
-        outs += [shape(s, F32) for s in (slab, packs[0].shape[-2:], packs[1].shape[-2:])]
-        out_specs += [vmem] * 3
-        scratch += [vm((GROUPS, LINE) + slab, BF)]
-        for s, held in ((slab, True), (packs[0].shape[-2:], False), (packs[1].shape[-2:], False)):
+        outs += [shape(s, F32) for s in (slab, slab, packs[0].shape[-2:], packs[1].shape[-2:])]
+        out_specs += [vmem] * 4
+        scratch += [vm((GROUPS, LINE) + slab, BF)] * 2
+        for s, held in ((slab, True), (slab, True), (packs[0].shape[-2:], False), (packs[1].shape[-2:], False)):
             bufs, sems = Reduce.scratch(s, nz, held)
             scratch += bufs + sems
     else:
-        outs += [shape((GROUPS, LINE) + slab, BF)]
-        out_specs += [vmem]
+        outs += [shape((GROUPS, LINE) + slab, BF)] * 2
+        out_specs += [vmem] * 2
         packs = []
     return pl.pallas_call(
         functools.partial(back_kernel, nz, masks, rows),
@@ -954,95 +1074,112 @@
         in_specs=in_specs,
         out_specs=out_specs,
         scratch_shapes=scratch,
-        compiler_params=pltpu.CompilerParams(collective_id=1, has_side_effects=True, vmem_limit_bytes=60 << 20),
+        compiler_params=pltpu.CompilerParams(collective_id=1, has_side_effects=True, vmem_limit_bytes=62 << 20),
         cost_estimate=pl.CostEstimate(flops=24_000_000_000, bytes_accessed=40_000_000, transcendentals=13_000_000),
         name="back",
-    )(tok, gmid, out_own, query, keys, values, firsts, wqkv, gain, gmixed, lse, delta, cos, sine, *packs)
-
-
-def pack_qkv(w_qkv, gain):
-    r = w_qkv.shape[0]
-    body = jnp.concatenate([w_qkv[:, :1152], w_qkv[:, 1152:]], 0)
-    return jnp.concatenate([body, jnp.pad(gain[:, None], ((0, r), (0, 127)))], 1)
-
-
-def pack_out(w_out, gain):
-    r = w_out.shape[0]
-    body = jnp.concatenate([w_out[:, :384], w_out[:, 384:]], 0)
-    return jnp.concatenate([body, jnp.pad(gain[:, None], ((0, r), (0, 127)))], 1)
-
-
-def unpack_rows(total):
-    r, c = total.shape[0] // 2, total.shape[1] - 128
-    return jnp.concatenate([total[:r, :c], total[r:, :c]], 1), total[:r, c]
-
-
-def pack_mlp(w_in, w_down):
-    parts = (w_in[:, 0], w_in[:, 1], w_down.T)
-    pads = jnp.zeros((w_in.shape[0], 128 - 3 * REST), BF)
-    return jnp.concatenate([x[:, :MAIN] for x in parts] + [x[:, MAIN:] for x in parts] + [pads], 1)
-
-
-def unpack_mlp(total):
-    gate, up, down = [
-        jnp.concatenate([total[:, MAIN * i : MAIN * i + MAIN], total[:, 3 * MAIN + REST * i : 3 * MAIN + REST * i + REST]], 1)
-        for i in range(3)
-    ]
-    return jnp.stack([gate, up], 1), down.T
+    )(tok, gmid, out_own, query, kv, firsts, wqkv, gain, gmixed, lse, delta, cos, sine, *packs)
+
+
+def finish_kernel(out, gtok, s0, s1, so, sm, out_o, gtok_o, qkv_o, w_out_o, gains_o, gate_o, down_o):
+    out_o[...] = out[...]
+    gtok_o[...] = gtok[...]
+    for i, total in enumerate((s0, s1)):
+        q, k, v0, v1, tile = unpack_group(total[...])
+        for j, x in enumerate((q, k)):
+            qkv_o[:, WIDTH * j + HALF * i : WIDTH * j + HALF * i + HALF] = x
+        at = 2 * WIDTH + HALF * i
+        qkv_o[:, at : at + 256] = v0
+        qkv_o[:, at + 256 : at + HALF] = v1
+    w_out_o[:, :HALF] = so[:SLIVER, :HALF]
+    w_out_o[:, HALF:] = so[SLIVER:, :HALF]
+    zeros = jnp.zeros((128 - SLIVER, 128), F32)
+    for i, col in enumerate((tile, so[:SLIVER, HALF:])):
+        gains_o[i : i + 1, :] = jnp.concatenate([col, zeros], 0).T[:1]
+    gate, up, down = unpack_mlp(sm[...])
+    gate_o[:, :SHARE] = gate
+    gate_o[:, SHARE:] = up
+    down_o[...] = down.T
+
+
+def finish(out, gtok, s0, s1, so, sm):
+    shape = jax.ShapeDtypeStruct
+    vmem = pl.BlockSpec(memory_space=pltpu.VMEM)
+    return pl.pallas_call(
+        finish_kernel,
+        out_shape=[
+            shape(out.shape, BF),
+            shape(gtok.shape, BF),
+            shape((SLIVER, 3 * WIDTH), F32),
+            shape((SLIVER, WIDTH), F32),
+            shape((8, 128), F32),
+            shape((BAND, 2 * SHARE), F32),
+            shape((SHARE, BAND), F32),
+        ],
+        in_specs=[vmem] * 6,
+        out_specs=[vmem] * 7,
+        compiler_params=pltpu.CompilerParams(vmem_limit_bytes=40 << 20),
+        name="finish",
+    )(out, gtok, s0, s1, so, sm)
 
 
 def whole_packs(w_qkv, w_out, attn_gain, mlp_gain, w_in, w_down):
     both = ("dp", "seq")
 
-    def rows_of(w, gain, pack):
-        w, gain = lax.all_gather(w, both, axis=0, tiled=True), lax.all_gather(gain, both, axis=0, tiled=True)
-        shards = jax.vmap(pack)(w.reshape(GROUPS * LINE, SLIVER, -1), gain.reshape(GROUPS * LINE, SLIVER))
-        return shards.reshape((GROUPS, LINE) + shards.shape[1:])
-
-    mlp = pack_mlp(lax.all_gather(w_in, "dp", axis=0, tiled=True), lax.all_gather(w_down, "dp", axis=1, tiled=True))
-    mlp = lax.all_gather(mlp, "seq", axis=0, tiled=False)
+    def shards_of(w):
+        w = lax.all_gather(w, both, axis=0, tiled=True)
+        return w.reshape(GROUPS * LINE, SLIVER, -1)
+
+    def slabs(pack, w, gain):
+        found = jax.vmap(pack)(w, jnp.pad(gain, ((0, 0), (0, 0), (0, 127))))
+        return found.reshape((GROUPS, LINE) + found.shape[1:])
+
+    qkv, gain_a, gain_m = shards_of(w_qkv), shards_of(attn_gain), shards_of(mlp_gain)
+    groups = [slabs(lambda w, t, i=i: pack_group(w, t, i), qkv, gain_a) for i in range(2)]
+    w_in, w_down = lax.all_gather(w_in, "dp", axis=0, tiled=True), lax.all_gather(w_down, "dp", axis=1, tiled=True)
+    mlp = lax.all_gather(pack_mlp(w_in[:, 0], w_in[:, 1], w_down.T), "seq", axis=0, tiled=False)
     mlp = mlp.reshape(LINE, GROUPS, BAND, -1).transpose(1, 0, 2, 3)
-    return rows_of(w_qkv, attn_gain, pack_qkv), rows_of(w_out, mlp_gain, pack_out), mlp
-
-
-def whole_sums(pq_g, po_g, pm_g):
+    return groups, slabs(pack_out, shards_of(w_out), gain_m), mlp
+
+
+def whole_sums(p0_g, p1_g, po_g, pm_g):
     both = ("dp", "seq")
-    found = []
-    for pack in (pq_g, po_g):
-        w, gain = jax.vmap(unpack_rows)(pack.reshape((GROUPS * LINE,) + pack.shape[2:]).astype(F32))
-        found.append(lax.psum_scatter(w.reshape(WIDTH, -1), both, scatter_dimension=0, tiled=True))
-        found.append(lax.psum_scatter(gain.reshape(WIDTH), both, scatter_dimension=0, tiled=True))
+
+    def scattered(x):
+        return lax.psum_scatter(x.reshape(WIDTH, -1), both, scatter_dimension=0, tiled=True)
+
+    parts = [jax.vmap(unpack_group)(p.reshape((GROUPS * LINE,) + p.shape[2:]).astype(F32)) for p in (p0_g, p1_g)]
+    columns = [parts[0][0], parts[1][0], parts[0][1], parts[1][1], parts[0][2], parts[0][3], parts[1][2], parts[1][3]]
+    g_qkv, gain_a = scattered(jnp.concatenate(columns, -1)), scattered(parts[1][4][..., :1])[:, 0]
+    po = po_g.reshape(GROUPS * LINE, 2 * SLIVER, -1).astype(F32)
+    g_out = scattered(jnp.concatenate([po[:, :SLIVER, :HALF], po[:, SLIVER:, :HALF]], -1))
+    gain_m = scattered(po[:, :SLIVER, HALF : HALF + 1])[:, 0]
     mlp = pm_g.astype(F32).transpose(1, 0, 2, 3).reshape(LINE, WIDTH, -1)
     mlp = lax.psum_scatter(mlp, "seq", scatter_dimension=0, tiled=False)
-    mlp = lax.psum_scatter(mlp, "dp", scatter_dimension=0, tiled=True)
-    return found + list(unpack_mlp(mlp))
+    gate, up, down = unpack_mlp(lax.psum_scatter(mlp, "dp", scatter_dimension=0, tiled=True))
+    return g_qkv, g_out, gain_a, gain_m, jnp.stack([gate, up], 1), down.T
 
 
 def on_device(tokens, w_qkv, w_out, attn_gain, mlp_gain, w_in, w_down, grad_out, *, dp, nz):
     rows = tokens.shape[0]
-    masks = (dp // 2, dp // 4, 1) if dp == GROUPS and nz == LINE else None
+    masks = (dp // 2, dp // 4, 1) if dp == GROUPS else None
     cos, sine = [jnp.asarray(t).reshape(nz, rows, 128) for t in rope_tables(nz * rows)]
     if masks:
-        packs = [pack_qkv(w_qkv, attn_gain), pack_out(w_out, mlp_gain), pack_mlp(w_in, w_down)]
-        got = front(tokens, grad_out, packs, cos, sine, nz, masks)
+        gains = jnp.pad(jnp.stack([attn_gain, mlp_gain]).astype(F32), ((0, 6), (0, 128 - SLIVER)))
+        weights = [w_qkv, w_out, gains, w_in.reshape(w_in.shape[0], -1), w_down]
+        got = front(tokens, grad_out, weights, cos, sine, nz, masks)
         po_all, pm_all = got[-2:]
     else:
-        pq_all, po_all, pm_all = whole_packs(w_qkv, w_out, attn_gain, mlp_gain, w_in, w_down)
-        got = front(tokens, grad_out, [pq_all], cos, sine, nz, None)
-    mixed, lse, query, gain, tok_own, gout_own, keys, values, firsts, wqkv = got[:10]
+        groups, po_all, pm_all = whole_packs(w_qkv, w_out, attn_gain, mlp_gain, w_in, w_down)
+        got = front(tokens, grad_out, groups, cos, sine, nz, None)
+    mixed, lse, query, gain, tok_own, gout_own, kv, firsts, wqkv = got[:9]
     out_own, gmid, gmixed, delta, po_g, pm_g = middle(tok_own, mixed, gout_own, po_all, pm_all)
-    found = back(
-        tok_own, gmid, out_own, query, keys, values, firsts, wqkv, gain, gmixed, lse, delta, cos, sine, [po_g, pm_g], nz, masks
-    )
-    gtok, out = found[:2]
-    if masks:
-        sq, so, sm = found[2:]
-        g_qkv, g_gain_a = unpack_rows(sq)
-        g_out, g_gain_m = unpack_rows(so)
-        g_in, g_down = unpack_mlp(sm)
-    else:
-        g_qkv, g_gain_a, g_out, g_gain_m, g_in, g_down = whole_sums(found[2], po_g, pm_g)
-    return out, gtok, g_qkv, g_out, g_gain_a, g_gain_m, g_in, g_down
+    found = back(tok_own, gmid, out_own, query, kv, firsts, wqkv, gain, gmixed, lse, delta, cos, sine, [po_g, pm_g], nz, masks)
+    gtok, out, *sums = found
+    if not masks:
+        return (out, gtok, *whole_sums(*sums, po_g, pm_g))
+    out, gtok, g_qkv, g_out, gains, g_in, g_down = finish(out, gtok, *sums)
+    g_in = g_in.reshape(g_in.shape[0], 2, SHARE)
+    return out, gtok, g_qkv, g_out, gains[0, :SLIVER], gains[1, :SLIVER], g_in, g_down
 
 
 def solution(mesh):

time: 254 us -> 250 us (0.984); the launches traced: 253 us -> 246 us
  local copies, waits for them, and re-layouts: 16.2 us -> 9.11 us
    pallas_call x1, Pallas kernels: 97.9 us -> 84.2 us  [front(): pl.pallas_call(functools.partial(front_kernel, nz, masks, rows), out_shap...]
    slice x15 -> x0, local copies, waits for them, and re-layouts: 9.42 us -> none  [the longest x4 4.54 us: unpack_rows(): return (jnp.concatenate([total[:r, :c], total[r:, :c]], 1), total[:r, c])]
    pallas_call x1, Pallas kernels: 28.2 us -> 37.5 us  [middle(): pl.pallas_call(functools.partial(middle_kernel, rows), out_shape=[shape((...]
    pallas_call x1, Pallas kernels: 107 us -> 111 us  [back(): pl.pallas_call(functools.partial(back_kernel, nz, masks, rows), out_shape...]
    reshape x0 -> x2, local copies, waits for them, and re-layouts: none -> 2.66 us  [the longest x1 1.71 us: on_device(): weights = [w_qkv, w_out, gains, w_in.reshape(w_in.shape[0], -1), w_down]]
    concatenate x4 -> x0, other arithmetic: 2.63 us -> none  [the longest x2 1.34 us: unpack_rows(): return (jnp.concatenate([total[:r, :c], total[r:, :c]], 1), total[:r, c])]
    unnamed x9 -> x12, local copies, waits for them, and re-layouts: 4.46 us -> 5.93 us
where the time goes in v3:
time: 250 us; the launch traced here: 246 us
  Pallas kernels  234 us (94%)
  local copies, waits for them, and re-layouts  9.11 us (4%)
    pallas_call x1, Pallas kernels, back(): pl.pallas_call(functools.partial(back_kernel, nz, masks, rows), out_shape...  111 us
    pallas_call x1, Pallas kernels, front(): pl.pallas_call(functools.partial(front_kernel, nz, masks, rows), out_shap...  84.2 us
    pallas_call x1, Pallas kernels, middle(): pl.pallas_call(functools.partial(middle_kernel, rows), out_shape=[shape((...  37.5 us
    unnamed x12, local copies, waits for them, and re-layouts  5.93 us

profile of v3, /device:TPU:0, one launch (start us, length us, event | category | flops | bytes accessed | tf_op | source)
XLA Modules:
  0.0 245.7 jit_solution(8588675699890170961)
XLA Ops:
  0.6 1.3 fusion.6.refs_4_
  1.9 1.7 reshape.28.refs_5_
  3.6 84.2 %front.1 = (bf16[512,768]{1,0:T(8,128)(2,1)}, f32[16,512]{1,0:T(8,128)}, bf16[512,768]{1,0:T(8,128)(2,1)}, f32[8,768]{1,0:T(8,128)}, bf16[512,768]{1,0:T(8,128)(...) custom-call(bf16[512,768]{1,0:T(8,128)(2,1)} %refs_0_.1, ...), custom_call_target="tpu_custom_call" | custom-call | flops 14000000000 | bytes 40000000 | tf_op jit(solution)/shard_map/front/pallas_call | solution.py:517
  87.8 37.5 %middle.1 = (bf16[512,768]{1,0:T(8,128)(2,1)}, f32[512,768]{1,0:T(8,128)}, bf16[512,768]{1,0:T(8,128)(2,1)}, f32[16,512]{1,0:T(8,128)}, bf16[8,4,48,512]{3,2,1,0...) custom-call(bf16[512,768]{1,0:T(8,128)(2,1)} %get-tuple-element.38.tok.refs_0_, bf16[512,768]{1,0:T(8,128)(2,1)} %get-tuple-element.39.mixed, ...), custom_call_target="tpu_custom_call" | custom-call | flops 11000000512 | bytes 25000000 | tf_op jit(solution)/shard_map/middle/pallas_call | solution.py:650
  125.3 111.0 %back.1 = (bf16[512,768]{1,0:T(8,128)(2,1)}, bf16[512,768]{1,0:T(8,128)(2,1)}, f32[48,640]{1,0:T(8,128)}, f32[48,640]{1,0:T(8,128)}, f32[48,512]{1,0:T(8,128)}, /*index=5*/f32[96,896]{1,0:T(8,128)}) custom-call(bf16[512,768]{1,0:T(8,128)(2,1)} %get-tuple-element.38.tok.refs_0_, f32[512,768]{1,0:T(8,128)} %get-tuple-element.43.refs_1_, ...), custom_call_target="tpu_custom_call" | custom-call | flops 24000000000 | bytes 40000000 | tf_op jit(solution)/shard_map/back/pallas_call | solution.py:1071
  236.4 0.0 copy-start
  236.4 1.1 copy-done
  237.5 0.0 copy-start.1
  237.5 1.1 copy-done.1
  238.6 0.0 copy-start.2
  238.6 1.0 copy-done.2
  239.6 0.0 copy-start.3
  239.6 0.9 copy-done.3
  240.5 0.0 copy-start.4
  240.5 0.9 copy-done.4
  241.4 0.0 copy-start.5
  241.4 0.9 copy-done.5
  242.3 1.5 finish.1
  243.8 0.5 slice_bitcast_fusion
  244.3 0.9 reshape.31
Async XLA Ops:
  236.4 1.1 copy-start
  237.5 1.1 copy-start.1
  238.6 1.0 copy-start.2
  239.6 0.9 copy-start.3
  240.5 0.9 copy-start.4
  241.4 0.9 copy-start.5
